TPU v7x, 256 devices: a whole 4x4x8 slice. The times are simulated.
256 devices in a mesh: ctx: 64 (over y, x, z_hi, core), tp: 4 (over z_lo).
Axes of the slice: x: 4, y: 4, z: 8 (z_hi: 2, z_lo: 4; z = z_hi * 4 + z_lo), core: 2. Of those that a mesh axis runs over, the one named last changes fastest.
Arguments:
- query_proj: bfloat16 [16384, 1024], P('ctx', 'tp'), may hold values from -4 to 4
- key_proj: bfloat16 [16384, 1024], P('ctx', 'tp'), may hold values from -4 to 4
- value_proj: bfloat16 [16384, 1024], P('ctx', 'tp'), may hold values from -4 to 4
- filter_taps: float32 [16384, 1024], P('ctx', 'tp'), may hold values from -1.5 to 1.5
- skip_bias: float32 [1024], P('tp'), may hold values from -2.5 to 2.5
- cotangent: bfloat16 [16384, 1024], P('ctx', 'tp'), may hold values from -4 to 4
Outputs:
- gated: bfloat16 [16384, 1024], P('ctx', 'tp')
- grad_query: bfloat16 [16384, 1024], P('ctx', 'tp')
- grad_key: bfloat16 [16384, 1024], P('ctx', 'tp')
- grad_value: bfloat16 [16384, 1024], P('ctx', 'tp')
- grad_taps: float32 [16384, 1024], P('ctx', 'tp')
- grad_skip: float32 [1024], P('tp')
All inputs are finite; a program needn't handle non-finite values.
Results may differ from a plain program's by a relative error of at most 0.001.
Values sent between devices are 32-bit elements; how exact they have to be, the bound alone decides.
A program may use at most 128 MiB of HBM per device.

v0:
```python
import math

import jax
import jax.numpy as jnp
from jax import lax
from jax.sharding import PartitionSpec as P

highest = lax.Precision.HIGHEST


def phase_table(count_rows, count_cols, col_start, modulus):
    row_ids = lax.iota(jnp.int32, count_rows)[:, None]
    col_ids = lax.iota(jnp.int32, count_cols)[None, :] + col_start
    angles = (row_ids * col_ids % modulus).astype(jnp.float32) * (2.0 * math.pi / modulus)
    return (jnp.cos(angles), jnp.sin(angles))


def contract(table, data, form):
    return jnp.einsum(form, table, data, precision=highest)


def fourier_axis(real_part, imag_part, sign):
    lead_count = real_part.shape[0]
    count = real_part.shape[1]
    tail_count = real_part.shape[2]
    factor = math.gcd(count, 64)
    if count <= 64 or factor == 1:
        cosine, sine_part = phase_table(count, count, 0, count)
        out_real = contract(cosine, real_part, "km,pmq->pkq")
        out_imag = contract(sine_part, real_part, "km,pmq->pkq") * sign
        out_real = out_real - sign * contract(sine_part, imag_part, "km,pmq->pkq")
        out_imag = out_imag + contract(cosine, imag_part, "km,pmq->pkq")
        return (out_real, out_imag)
    inner = count // factor

    def regroup(array):
        return array.reshape(lead_count, inner, factor * tail_count)

    first_real, first_imag = fourier_axis(regroup(real_part), regroup(imag_part), sign)
    first_real = first_real.reshape(lead_count, inner, factor, tail_count)
    first_imag = first_imag.reshape(lead_count, inner, factor, tail_count)
    twist_cos, twist_sin = phase_table(inner, factor, 0, count)
    twist_cos = twist_cos[None, :, :, None]
    twist_sin = twist_sin[None, :, :, None]
    turned_real = first_real * twist_cos - sign * first_imag * twist_sin
    turned_imag = first_imag * twist_cos + sign * first_real * twist_sin
    last_real, last_imag = fourier_axis(
        turned_real.reshape(lead_count * inner, factor, tail_count),
        turned_imag.reshape(lead_count * inner, factor, tail_count),
        sign,
    )

    def reorder(array):
        return jnp.transpose(
            array.reshape(lead_count, inner, factor, tail_count), (0, 2, 1, 3)
        ).reshape(lead_count, count, tail_count)

    return (reorder(last_real), reorder(last_imag))


def forward_transform(fields):
    devices_ctx = lax.axis_size("ctx")
    kernel_extent = fields.shape[1]
    stride = kernel_extent // devices_ctx
    period = 2 * kernel_extent * devices_ctx
    position = lax.axis_index("ctx")
    column_block = lax.all_to_all(fields[:, None], "ctx", split_axis=2, concat_axis=1, tiled=True)
    cosine, sine_part = phase_table(2 * devices_ctx, devices_ctx, 0, 2 * devices_ctx)
    real_part = contract(cosine, column_block, "kn,fnsc->fksc")
    imag_part = -contract(sine_part, column_block, "kn,fnsc->fksc")
    twist_cos, twist_sin = phase_table(2 * devices_ctx, stride, position * stride, period)
    twist_cos = twist_cos[None, :, :, None]
    twist_sin = twist_sin[None, :, :, None]
    real_in = lax.all_to_all(
        real_part * twist_cos + imag_part * twist_sin,
        "ctx",
        split_axis=1,
        concat_axis=2,
        tiled=True,
    )
    imag_in = lax.all_to_all(
        imag_part * twist_cos - real_part * twist_sin,
        "ctx",
        split_axis=1,
        concat_axis=2,
        tiled=True,
    )
    shape = real_in.shape
    flat = (shape[0] * shape[1], shape[2], shape[3])
    out_real, out_imag = fourier_axis(real_in.reshape(flat), imag_in.reshape(flat), -1)
    return (out_real.reshape(shape), out_imag.reshape(shape))


def inverse_transform(real_in, imag_in):
    devices_ctx = lax.axis_size("ctx")
    shape = real_in.shape
    kernel_extent = shape[2]
    stride = kernel_extent // devices_ctx
    period = 2 * kernel_extent * devices_ctx
    position = lax.axis_index("ctx")
    flat = (shape[0] * shape[1], shape[2], shape[3])
    time_real, time_imag = fourier_axis(real_in.reshape(flat), imag_in.reshape(flat), 1)
    time_real = time_real.reshape(shape)
    time_imag = time_imag.reshape(shape)
    part_real = lax.all_to_all(time_real, "ctx", split_axis=2, concat_axis=1, tiled=True)
    part_imag = lax.all_to_all(time_imag, "ctx", split_axis=2, concat_axis=1, tiled=True)
    twist_cos, twist_sin = phase_table(2 * devices_ctx, stride, position * stride, period)
    twist_cos = twist_cos[None, :, :, None]
    twist_sin = twist_sin[None, :, :, None]
    turned_real = part_real * twist_cos - part_imag * twist_sin
    turned_imag = part_imag * twist_cos + part_real * twist_sin
    back_cos, back_sin = phase_table(devices_ctx, 2 * devices_ctx, 0, 2 * devices_ctx)
    summed = contract(back_cos, turned_real, "nk,fksc->fnsc") - contract(
        back_sin, turned_imag, "nk,fksc->fnsc"
    )
    blocks = summed * (1.0 / period)
    series = lax.all_to_all(blocks, "ctx", split_axis=1, concat_axis=2, tiled=True)
    return series[:, 0]


def spectral_products(input_real, input_imag, taps_real, taps_imag, grad_real, grad_imag):
    conv_real = input_real * taps_real - input_imag * taps_imag
    conv_imag = input_real * taps_imag + input_imag * taps_real
    back_real = taps_real * grad_real + taps_imag * grad_imag
    back_imag = taps_real * grad_imag - taps_imag * grad_real
    tapg_real = input_real * grad_real + input_imag * grad_imag
    tapg_imag = input_real * grad_imag - input_imag * grad_real
    return (conv_real, conv_imag, back_real, back_imag, tapg_real, tapg_imag)


def shards(query_proj, key_proj, value_proj, filter_taps, skip_bias, cotangent):
    query32 = query_proj.astype(jnp.float32)
    key32 = key_proj.astype(jnp.float32)
    value32 = value_proj.astype(jnp.float32)
    cot32 = cotangent.astype(jnp.float32)
    inputs = key32 * value32
    grad_conv = cot32 * query32
    spec_real, spec_imag = forward_transform(jnp.stack([inputs, filter_taps]))
    conv_real = spec_real[0] * spec_real[1] - spec_imag[0] * spec_imag[1]
    conv_imag = spec_real[0] * spec_imag[1] + spec_imag[0] * spec_real[1]
    conv_out = inverse_transform(conv_real[None], conv_imag[None])[0]
    grad_real, grad_imag = forward_transform(grad_conv[None])
    unused_real, unused_imag, back_real, back_imag, tapg_real, tapg_imag = spectral_products(
        spec_real[0], spec_imag[0], spec_real[1], spec_imag[1], grad_real[0], grad_imag[0]
    )
    results = inverse_transform(
        jnp.stack([back_real, tapg_real]), jnp.stack([back_imag, tapg_imag])
    )
    conv_back = results[0]
    taps_back = results[1]
    mixed = conv_out + skip_bias * inputs
    gated = (query32 * mixed).astype(jnp.bfloat16)
    grad_query = (cot32 * mixed).astype(jnp.bfloat16)
    grad_inputs = conv_back + skip_bias * grad_conv
    grad_key = (grad_inputs * value32).astype(jnp.bfloat16)
    grad_value = (grad_inputs * key32).astype(jnp.bfloat16)
    grad_scale = 1.0 / math.sqrt(inputs.shape[0] * lax.axis_size("ctx"))
    grad_taps = taps_back * grad_scale
    grad_skip = lax.psum(jnp.sum(grad_conv * inputs, axis=0), "ctx") * grad_scale
    return (gated, grad_query, grad_key, grad_value, grad_taps, grad_skip)


def solution(mesh):
    in_specs = (
        P("ctx", "tp"),
        P("ctx", "tp"),
        P("ctx", "tp"),
        P("ctx", "tp"),
        P("tp"),
        P("ctx", "tp"),
    )
    out_specs = (
        P("ctx", "tp"),
        P("ctx", "tp"),
        P("ctx", "tp"),
        P("ctx", "tp"),
        P("ctx", "tp"),
        P("tp"),
    )
    return jax.shard_map(shards, mesh=mesh, in_specs=in_specs, out_specs=out_specs, check_vma=False)
```

profile of v0, /device:TPU:33, one launch (start us, length us, event | category | flops | bytes accessed | tf_op | source)
XLA Modules:
  0.0 579.0 jit_solution(15482393662807741955)
XLA Ops:
  2.6 14.0 %all-to-all-start.6 = ((f32[1,1,256,256]{3,1,0,2:T(1,128)}), f32[1,1,256,256]{3,1,0,2:T(1,128)S(1)}, u32[]{:S(2)}, u32[]{:S(2)}) async-start(f32[1,1,256,256]{3,1,0,2:T(1,128)} %copy.124), calls=%async_computation.6 | async-start | bytes 524288 | tf_op jit(solution)/shard_map/all_to_all | solution.py:67
  18.8 14.5 %all-to-all-done.6 = f32[1,1,256,256]{3,1,0,2:T(1,128)S(1)} async-done(((f32[1,1,256,256]{3,1,0,2:T(1,128)}), f32[1,1,256,256]{3,1,0,2:T(1,128)S(1)}, u32[]{:S(2)}, u32[]{:S(2)}) %all-to-all-start.6) | async-done | bytes 262176 | tf_op jit(solution)/shard_map/all_to_all | solution.py:67
  33.3 4.5 all-to-all-start
  41.8 16.7 %all-to-all-done = f32[2,1,256,256]{3,0,1,2:T(2,128)S(1)} async-done(((f32[2,1,256,256]{3,0,1,2:T(2,128)}), f32[2,1,256,256]{3,0,1,2:T(2,128)S(1)}, u32[]{:S(2)}, u32[]{:S(2)}) %all-to-all-start) | async-done | bytes 524320 | tf_op jit(solution)/shard_map/all_to_all | solution.py:67
  58.6 4.5 all-to-all-start.7
  64.1 17.1 %all-to-all-done.7 = f32[1,128,4,256]{3,2,0,1:T(4,128)S(1)} async-done(((f32[1,128,4,256]{3,2,0,1:T(4,128)}), f32[1,128,4,256]{3,2,0,1:T(4,128)S(1)}, u32[]{:S(2)}, u32[]{:S(2)}) %all-to-all-start.7) | async-done | bytes 524320 | tf_op jit(solution)/shard_map/all_to_all | solution.py:74
  81.2 5.6 all-to-all-start.8
  92.0 12.1 %all-to-all-done.8 = f32[1,128,4,256]{3,2,0,1:T(4,128)} async-done(((f32[1,128,4,256]{3,2,0,1:T(4,128)}), f32[1,128,4,256]{3,2,0,1:T(4,128)}, u32[]{:S(2)}, u32[]{:S(2)}) %all-to-all-start.8) | async-done | bytes 524320 | tf_op jit(solution)/shard_map/all_to_all | solution.py:81
  104.2 4.5 all-to-all-start.1
  114.6 23.4 %all-to-all-done.1 = f32[2,128,4,256]{3,2,0,1:T(4,128)S(1)} async-done(((f32[2,128,4,256]{3,2,0,1:T(4,128)}), f32[2,128,4,256]{3,2,0,1:T(4,128)S(1)}, u32[]{:S(2)}, u32[]{:S(2)}) %all-to-all-start.1) | async-done | bytes 1048608 | tf_op jit(solution)/shard_map/all_to_all | solution.py:74
  138.0 5.6 all-to-all-start.2
  154.2 2.9 fusion.155
  159.1 11.9 %all-to-all-done.2 = f32[2,128,4,256]{3,2,0,1:T(4,128)} async-done(((f32[2,128,4,256]{3,2,0,1:T(4,128)}), f32[2,128,4,256]{3,2,0,1:T(4,128)}, u32[]{:S(2)}, u32[]{:S(2)}) %all-to-all-start.2) | async-done | bytes 1048608 | tf_op jit(solution)/shard_map/all_to_all | solution.py:81
  175.4 3.5 fusion.4
  180.9 3.0 fusion.2
  192.9 2.9 fusion.27
  208.9 2.9 fusion.8
  216.1 5.7 all-to-all-start.3
  228.8 9.6 %all-to-all-done.3 = f32[1,2,256,256]{3,1,0,2:T(2,128)} async-done(((f32[1,2,256,256]{3,1,0,2:T(2,128)}), f32[1,2,256,256]{3,1,0,2:T(2,128)}, u32[]{:S(2)}, u32[]{:S(2)}) %all-to-all-start.3) | async-done | bytes 524320 | tf_op jit(solution)/shard_map/all_to_all | solution.py:105
  238.4 5.9 %all-to-all-start.4 = ((f32[1,2,256,256]{3,1,0,2:T(2,128)}), f32[1,2,256,256]{3,1,0,2:T(2,128)}, u32[]{:S(2)}, u32[]{:S(2)}) async-start(f32[1,2,256,256]{3,1,0,2:T(2,128)} %bitcast.308), calls=%async_computation.4 | async-start | bytes 1048576 | tf_op jit(solution)/shard_map/all_to_all | solution.py:106
  244.3 2.9 fusion.135
  247.9 3.2 fusion
  256.6 3.0 copy.136
  261.5 11.3 %all-to-all-start.9 = ((f32[2,2,256,256]{3,1,0,2:T(2,128)}), f32[2,2,256,256]{3,1,0,2:T(2,128)S(1)}, u32[]{:S(2)}, u32[]{:S(2)}) async-start(f32[2,2,256,256]{3,1,0,2:T(2,128)} %copy.136), calls=%async_computation.9 | async-start | bytes 2097152 | tf_op jit(solution)/shard_map/all_to_all | solution.py:105
  278.3 22.7 %all-to-all-done.9 = f32[2,2,256,256]{3,1,0,2:T(2,128)S(1)} async-done(((f32[2,2,256,256]{3,1,0,2:T(2,128)}), f32[2,2,256,256]{3,1,0,2:T(2,128)S(1)}, u32[]{:S(2)}, u32[]{:S(2)}) %all-to-all-start.9) | async-done | bytes 1048608 | tf_op jit(solution)/shard_map/all_to_all | solution.py:105
  301.1 4.5 all-to-all-start.10
  313.5 20.4 %all-to-all-done.10 = f32[2,2,256,256]{3,1,0,2:T(2,128)S(1)} async-done(((f32[2,2,256,256]{3,1,0,2:T(2,128)}), f32[2,2,256,256]{3,1,0,2:T(2,128)S(1)}, u32[]{:S(2)}, u32[]{:S(2)}) %all-to-all-start.10) | async-done | bytes 1048608 | tf_op jit(solution)/shard_map/all_to_all | solution.py:106
  334.0 4.8 all-to-all-start.5
  343.6 9.1 %all-to-all-done.5 = f32[1,64,4,256]{3,2,0,1:T(4,128)S(1)} async-done(((f32[1,64,4,256]{3,2,0,1:T(4,128)}), f32[1,64,4,256]{3,2,0,1:T(4,128)S(1)}, u32[]{:S(2)}, u32[]{:S(2)}) %all-to-all-start.5) | async-done | bytes 262176 | tf_op jit(solution)/shard_map/all_to_all | solution.py:117
  352.7 4.5 all-to-all-start.11
  357.3 17.2 %all-to-all-done.11 = f32[2,64,4,256]{3,2,0,1:T(4,128)S(1)} async-done(((f32[2,64,4,256]{3,2,0,1:T(4,128)}), f32[2,64,4,256]{3,2,0,1:T(4,128)S(1)}, u32[]{:S(2)}, u32[]{:S(2)}) %all-to-all-start.11) | async-done | bytes 524320 | tf_op jit(solution)/shard_map/all_to_all | solution.py:117
  376.7 200.7 %psum.7 = f32[256]{0:T(256)S(1)} all-reduce(f32[256]{0:T(256)S(1)} %get-tuple-element.24), channel_id=1, replica_groups=mesh['ctx'=64,'tp'=4] {'ctx'}, use_global_device_ids=true, to_apply=%region_1.2 | all-reduce | flops 256 | bytes 2048 | tf_op jit(solution)/shard_map/psum | solution.py:159
  (130 shorter events, 102.0 us)
Async XLA Ops:
  2.6 14.0 %copy-start.5 = (bf16[256,256]{1,0:T(8,128)(2,1)S(1)}, bf16[256,256]{1,0:T(8,128)(2,1)}, u32[]{:S(2)}) copy-start(bf16[256,256]{1,0:T(8,128)(2,1)} %param.8) | copy-start | bytes 393220
  2.6 14.0 %copy-start.6 = (bf16[256,256]{1,0:T(8,128)(2,1)S(1)}, bf16[256,256]{1,0:T(8,128)(2,1)}, u32[]{:S(2)}) copy-start(bf16[256,256]{1,0:T(8,128)(2,1)} %param.7) | copy-start | bytes 393220
  2.6 30.7 %all-to-all-start.6 = ((f32[1,1,256,256]{3,1,0,2:T(1,128)}), f32[1,1,256,256]{3,1,0,2:T(1,128)S(1)}, u32[]{:S(2)}, u32[]{:S(2)}) async-start(f32[1,1,256,256]{3,1,0,2:T(1,128)} %copy.124), calls=%async_computation.6 | async-start | bytes 524288 | tf_op jit(solution)/shard_map/all_to_all | solution.py:67
  16.7 1.0 copy-start.9
  33.3 25.2 %all-to-all-start = ((f32[2,1,256,256]{3,0,1,2:T(2,128)}), f32[2,1,256,256]{3,0,1,2:T(2,128)S(1)}, u32[]{:S(2)}, u32[]{:S(2)}) async-start(f32[2,1,256,256]{3,0,1,2:T(2,128)} %copy.100), calls=%async_computation | async-start | bytes 1048576 | tf_op jit(solution)/shard_map/all_to_all | solution.py:67
  58.6 22.6 %all-to-all-start.7 = ((f32[1,128,4,256]{3,2,0,1:T(4,128)}), f32[1,128,4,256]{3,2,0,1:T(4,128)S(1)}, u32[]{:S(2)}, u32[]{:S(2)}) async-start(f32[1,128,4,256]{3,2,0,1:T(4,128)} %copy.127), calls=%async_computation.7 | async-start | bytes 1048576 | tf_op jit(solution)/shard_map/all_to_all | solution.py:74
  81.2 23.0 %all-to-all-start.8 = ((f32[1,128,4,256]{3,2,0,1:T(4,128)}), f32[1,128,4,256]{3,2,0,1:T(4,128)}, u32[]{:S(2)}, u32[]{:S(2)}) async-start(f32[1,128,4,256]{3,2,0,1:T(4,128)} %copy.129), calls=%async_computation.8 | async-start | bytes 1048576 | tf_op jit(solution)/shard_map/all_to_all | solution.py:81
  104.2 33.8 %all-to-all-start.1 = ((f32[2,128,4,256]{3,2,0,1:T(4,128)}), f32[2,128,4,256]{3,2,0,1:T(4,128)S(1)}, u32[]{:S(2)}, u32[]{:S(2)}) async-start(f32[2,128,4,256]{3,2,0,1:T(4,128)} %copy.103), calls=%async_computation.1 | async-start | bytes 2097152 | tf_op jit(solution)/shard_map/all_to_all | solution.py:74
  138.0 33.0 %all-to-all-start.2 = ((f32[2,128,4,256]{3,2,0,1:T(4,128)}), f32[2,128,4,256]{3,2,0,1:T(4,128)}, u32[]{:S(2)}, u32[]{:S(2)}) async-start(f32[2,128,4,256]{3,2,0,1:T(4,128)} %copy.106), calls=%async_computation.2 | async-start | bytes 2097152 | tf_op jit(solution)/shard_map/all_to_all | solution.py:81
  173.4 2.0 copy-start
  191.4 1.6 copy-start.2
  191.4 1.6 copy-start.3
  204.2 1.5 copy-start.1
  216.1 22.3 %all-to-all-start.3 = ((f32[1,2,256,256]{3,1,0,2:T(2,128)}), f32[1,2,256,256]{3,1,0,2:T(2,128)}, u32[]{:S(2)}, u32[]{:S(2)}) async-start(f32[1,2,256,256]{3,1,0,2:T(2,128)} %bitcast.311), calls=%async_computation.3 | async-start | bytes 1048576 | tf_op jit(solution)/shard_map/all_to_all | solution.py:105
  238.4 23.1 %all-to-all-start.4 = ((f32[1,2,256,256]{3,1,0,2:T(2,128)}), f32[1,2,256,256]{3,1,0,2:T(2,128)}, u32[]{:S(2)}, u32[]{:S(2)}) async-start(f32[1,2,256,256]{3,1,0,2:T(2,128)} %bitcast.308), calls=%async_computation.4 | async-start | bytes 1048576 | tf_op jit(solution)/shard_map/all_to_all | solution.py:106
  261.5 39.6 %all-to-all-start.9 = ((f32[2,2,256,256]{3,1,0,2:T(2,128)}), f32[2,2,256,256]{3,1,0,2:T(2,128)S(1)}, u32[]{:S(2)}, u32[]{:S(2)}) async-start(f32[2,2,256,256]{3,1,0,2:T(2,128)} %copy.136), calls=%async_computation.9 | async-start | bytes 2097152 | tf_op jit(solution)/shard_map/all_to_all | solution.py:105
  301.1 32.9 %all-to-all-start.10 = ((f32[2,2,256,256]{3,1,0,2:T(2,128)}), f32[2,2,256,256]{3,1,0,2:T(2,128)S(1)}, u32[]{:S(2)}, u32[]{:S(2)}) async-start(f32[2,2,256,256]{3,1,0,2:T(2,128)} %copy.141), calls=%async_computation.10 | async-start | bytes 2097152 | tf_op jit(solution)/shard_map/all_to_all | solution.py:106
  334.0 18.7 %all-to-all-start.5 = ((f32[1,64,4,256]{3,2,0,1:T(4,128)}), f32[1,64,4,256]{3,2,0,1:T(4,128)S(1)}, u32[]{:S(2)}, u32[]{:S(2)}) async-start(f32[1,64,4,256]{3,2,0,1:T(4,128)} %copy.123), calls=%async_computation.5 | async-start | bytes 524288 | tf_op jit(solution)/shard_map/all_to_all | solution.py:117
  352.7 21.8 %all-to-all-start.11 = ((f32[2,64,4,256]{3,2,0,1:T(4,128)}), f32[2,64,4,256]{3,2,0,1:T(4,128)S(1)}, u32[]{:S(2)}, u32[]{:S(2)}) async-start(f32[2,64,4,256]{3,2,0,1:T(4,128)} %copy.149), calls=%async_computation.11 | async-start | bytes 1048576 | tf_op jit(solution)/shard_map/all_to_all | solution.py:117
  374.6 0.9 copy-start.4
  374.7 1.0 copy-start.7
  374.7 1.0 copy-start.8
  374.7 1.0 copy-start.10
where the time goes:
time: 587 us; the launch traced here: 579 us
  blocking collectives  201 us (34%)
  waiting for transfers between devices  177 us (30%)
  starting transfers between devices  75.6 us (13%)
  matrix products  63.6 us (11%)
  local copies, waits for them, and re-layouts  53 us (9%)
  other arithmetic  7.82 us (1%)
    psum x1, blocking collectives, shards(): lax.psum(jnp.sum(grad_conv * inputs, axis=0), 'ctx') * grad_scale  201 us
    dot_general x40, matrix products, contract(): return jnp.einsum(form, table, data, precision=highest)  63.6 us
    all_to_all x2, waiting for transfers between devices, forward_transform(): lax.all_to_all(real_part * twist_cos + imag_part * twist_sin, 'ctx', spli...  40.5 us
    all_to_all x2, waiting for transfers between devices, inverse_transform(): lax.all_to_all(time_real, 'ctx', split_axis=2, concat_axis=1, tiled=True)  32.3 us
    all_to_all x2, waiting for transfers between devices, forward_transform(): lax.all_to_all(fields[:, None], 'ctx', split_axis=2, concat_axis=1, tiled...  31.2 us
    all_to_all x2, waiting for transfers between devices, inverse_transform(): lax.all_to_all(blocks, 'ctx', split_axis=1, concat_axis=2, tiled=True)  26.3 us
    all_to_all x2, waiting for transfers between devices, forward_transform(): lax.all_to_all(imag_part * twist_cos - real_part * twist_sin, 'ctx', spli...  24 us
    all_to_all x2, waiting for transfers between devices, inverse_transform(): lax.all_to_all(time_imag, 'ctx', split_axis=2, concat_axis=1, tiled=True)  22.3 us
  transfers between devices with their start and end apart: 12, of which 12 were waited for; matrix products, arithmetic and copies ran while one was open for 13% of the time, Pallas kernels for 0%

commit v1 on v0

v1 whole, which is shorter than its diff:
```python
import math

import jax
import jax.numpy as jnp
import numpy as np
from jax import lax
from jax.sharding import PartitionSpec as P

HI = lax.Precision.HIGH
HALF = 128


def tables():
    n = np.arange(HALF)
    k = np.arange(HALF) + 0.5
    period = 2 * HALF * HALF
    a1 = 2 * np.pi * np.outer(k, n) / (2 * HALF)
    at = 2 * np.pi * np.outer(k, n) / period
    a2 = 2 * np.pi * np.outer(n, np.arange(HALF)) / HALF
    c2, s2 = np.cos(a2), np.sin(a2)
    f1 = np.concatenate([np.cos(a1), -np.sin(a1)], 0)
    f2 = np.block([[c2, -s2], [s2, c2]])
    g2 = np.block([[c2, s2], [-s2, c2]])
    g1 = np.concatenate([np.cos(a1).T, -np.sin(a1).T], 1) * (2 / period)
    return [np.asarray(t, np.float32) for t in (f1, f2, g1, g2, np.cos(at), -np.sin(at))]


def shards(query_proj, key_proj, value_proj, filter_taps, skip_bias, cotangent):
    f1, f2, g1, g2, tr, ti = [jnp.asarray(t) for t in tables()]
    q = query_proj.astype(jnp.float32)
    k = key_proj.astype(jnp.float32)
    v = value_proj.astype(jnp.float32)
    ct = cotangent.astype(jnp.float32)
    u = k * v
    gc = ct * q
    n = lax.axis_size("ctx")
    rows, width = u.shape
    each = width // n

    def out(x):
        x = x.T.reshape(n, each, rows)
        x = lax.all_to_all(x, "ctx", split_axis=0, concat_axis=0, tiled=True)
        return jnp.transpose(x.reshape(n, each, rows // HALF, HALF), (1, 0, 2, 3)).reshape(each, HALF, HALF)

    def back(x):
        x = jnp.transpose(x.reshape(each, n, rows // HALF, HALF), (1, 0, 2, 3)).reshape(n, each, rows)
        x = lax.all_to_all(x, "ctx", split_axis=0, concat_axis=0, tiled=True)
        return x.reshape(width, rows).T

    def fwd(x):
        a = jnp.einsum("kn,cnm->ckm", f1, x, precision=HI)
        ar, ai = a[:, :HALF], a[:, HALF:]
        b = jnp.concatenate([ar * tr - ai * ti, ar * ti + ai * tr], 2)
        b = jnp.einsum("ckm,mj->ckj", b, f2, precision=HI)
        return b[..., :HALF], b[..., HALF:]

    def inv(r, i):
        d = jnp.einsum("ckm,mj->ckj", jnp.concatenate([r, i], 2), g2, precision=HI)
        dr, di = d[..., :HALF], d[..., HALF:]
        e = jnp.concatenate([dr * tr + di * ti, di * tr - dr * ti], 1)
        return jnp.einsum("nk,ckm->cnm", g1, e, precision=HI)

    ur, ui = fwd(out(u))
    hr, hi = fwd(out(filter_taps))
    gr, gi = fwd(out(gc))
    conv = back(inv(ur * hr - ui * hi, ur * hi + ui * hr))
    conv_back = back(inv(hr * gr + hi * gi, hr * gi - hi * gr))
    taps_back = back(inv(ur * gr + ui * gi, ur * gi - ui * gr))
    mixed = conv + skip_bias * u
    grad_inputs = conv_back + skip_bias * gc
    scale = 1.0 / math.sqrt(rows * n)
    grad_skip = lax.psum(jnp.sum(gc * u, axis=0), "ctx") * scale
    bf = jnp.bfloat16
    return (
        (q * mixed).astype(bf),
        (ct * mixed).astype(bf),
        (grad_inputs * v).astype(bf),
        (grad_inputs * k).astype(bf),
        taps_back * scale,
        grad_skip,
    )


def solution(mesh):
    s = P("ctx", "tp")
    return jax.shard_map(
        shards, mesh=mesh, in_specs=(s, s, s, s, P("tp"), s), out_specs=(s, s, s, s, s, P("tp")), check_vma=False
    )
```

time: 587 us -> 344 us (0.59)
  waiting for transfers between devices: 177 us -> 78.9 us
  matrix products: 63.6 us -> 5.53 us
  starting transfers between devices: 75.6 us -> 36.7 us
  local copies, waits for them, and re-layouts: 53 us -> 17.3 us
  other arithmetic: 7.82 us -> 1.58 us
    all_to_all x12 -> x6, waiting for transfers between devices: 177 us -> 78.9 us  [the longest x3 40.9 us: out(): x = lax.all_to_all(x, 'ctx', split_axis=0, concat_axis=0, tiled=True)]
    dot_general x40 -> x11, matrix products: 63.6 us -> 5.16 us  [the longest x3 1.84 us: fwd(): b = jnp.einsum('ckm,mj->ckj', b, f2, precision=HI)]
    all_to_all x12 -> x6, starting transfers between devices: 75.6 us -> 36.7 us  [the longest x3 23 us: out(): x = lax.all_to_all(x, 'ctx', split_axis=0, concat_axis=0, tiled=True)]
    another operation x15 -> x0, local copies, waits for them, and re-layouts: 13.6 us -> none  [the longest x6 5.74 us: regroup(): return array.reshape(lead_count, inner, factor * tail_count)]
    all_to_all x10 -> x0, local copies, waits for them, and re-layouts: 10.5 us -> none  [the longest x3 3.97 us: inverse_transform(): lax.all_to_all(time_real, 'ctx', split_axis=2, concat_axis=1, tiled=True)]
    unnamed x22 -> x33, local copies, waits for them, and re-layouts: 1.84 us -> 10.3 us
    reshape x12 -> x18, local copies, waits for them, and re-layouts: 12.6 us -> 6.74 us  [the longest x6 3.24 us: back(): jnp.transpose(x.reshape(each, n, rows // HALF, HALF), (1, 0, 2, 3))]
  transfers between devices with their start and end apart: 12 -> 6, of which waited for: 12 -> 6; matrix products, arithmetic and copies ran while one was open for 13% -> 2% of each run, Pallas kernels for 0% -> 0%
where the time goes in v1:
time: 344 us; the launch traced here: 342 us
  blocking collectives  201 us (58%)
  waiting for transfers between devices  78.9 us (23%)
  starting transfers between devices  36.7 us (11%)
  local copies, waits for them, and re-layouts  17.3 us (5%)
  matrix products  5.53 us (2%)
    psum x1, blocking collectives, shards(): grad_skip = lax.psum(jnp.sum(gc * u, axis=0), 'ctx') * scale  201 us
    all_to_all x3, waiting for transfers between devices, out(): x = lax.all_to_all(x, 'ctx', split_axis=0, concat_axis=0, tiled=True)  40.9 us
    all_to_all x3, waiting for transfers between devices, back(): x = lax.all_to_all(x, 'ctx', split_axis=0, concat_axis=0, tiled=True)  37.9 us
    all_to_all x3, starting transfers between devices, out(): x = lax.all_to_all(x, 'ctx', split_axis=0, concat_axis=0, tiled=True)  23 us
    all_to_all x3, starting transfers between devices, back(): x = lax.all_to_all(x, 'ctx', split_axis=0, concat_axis=0, tiled=True)  13.7 us
    unnamed x33, local copies, waits for them, and re-layouts  10.3 us
  transfers between devices with their start and end apart: 6, of which 6 were waited for; matrix products, arithmetic and copies ran while one was open for 2% of the time, Pallas kernels for 0%

profile of v1, /device:TPU:33, one launch (start us, length us, event | category | flops | bytes accessed | tf_op | source)
XLA Modules:
  0.0 341.8 jit_solution(7897791142426342409)
XLA Ops:
  0.6 1.0 copy.33
  1.8 0.8 reshape.78
  2.6 14.0 %all-to-all-start.3 = ((f32[64,4,256]{2,1,0:T(4,128)}), f32[64,4,256]{2,1,0:T(4,128)S(1)}, u32[]{:S(2)}, u32[]{:S(2)}) async-start(f32[64,4,256]{2,1,0:T(4,128)} %reshape.78), calls=%async_computation.3 | async-start | bytes 524288 | tf_op jit(solution)/shard_map/all_to_all | solution.py:42
  16.8 0.8 copy-done.10
  17.7 0.8 reshape.69
  18.5 14.9 %all-to-all-done.3 = f32[64,4,256]{2,1,0:T(4,128)S(1)} async-done(((f32[64,4,256]{2,1,0:T(4,128)}), f32[64,4,256]{2,1,0:T(4,128)S(1)}, u32[]{:S(2)}, u32[]{:S(2)}) %all-to-all-start.3) | async-done | bytes 262176 | tf_op jit(solution)/shard_map/all_to_all | solution.py:42
  33.4 4.5 %all-to-all-start = ((f32[64,4,256]{2,1,0:T(4,128)}), f32[64,4,256]{2,1,0:T(4,128)S(1)}, u32[]{:S(2)}, u32[]{:S(2)}) async-start(f32[64,4,256]{2,1,0:T(4,128)} %reshape.69), calls=%async_computation | async-start | bytes 524288 | tf_op jit(solution)/shard_map/all_to_all | solution.py:42
  38.0 0.8 reshape.72
  38.8 14.2 %all-to-all-done = f32[64,4,256]{2,1,0:T(4,128)S(1)} async-done(((f32[64,4,256]{2,1,0:T(4,128)}), f32[64,4,256]{2,1,0:T(4,128)S(1)}, u32[]{:S(2)}, u32[]{:S(2)}) %all-to-all-start) | async-done | bytes 262176 | tf_op jit(solution)/shard_map/all_to_all | solution.py:42
  53.0 4.5 %all-to-all-start.1 = ((f32[64,4,256]{2,1,0:T(4,128)}), f32[64,4,256]{2,1,0:T(4,128)S(1)}, u32[]{:S(2)}, u32[]{:S(2)}) async-start(f32[64,4,256]{2,1,0:T(4,128)} %reshape.72), calls=%async_computation.1 | async-start | bytes 524288 | tf_op jit(solution)/shard_map/all_to_all | solution.py:42
  58.1 0.8 copy-done.3
  59.7 11.9 %all-to-all-done.1 = f32[64,4,256]{2,1,0:T(4,128)S(1)} async-done(((f32[64,4,256]{2,1,0:T(4,128)}), f32[64,4,256]{2,1,0:T(4,128)S(1)}, u32[]{:S(2)}, u32[]{:S(2)}) %all-to-all-start.1) | async-done | bytes 262176 | tf_op jit(solution)/shard_map/all_to_all | solution.py:42
  72.0 0.8 copy-done.7
  73.9 0.7 copy-done.1
  75.2 0.6 fusion.4
  76.7 0.8 copy-done
  79.0 0.7 copy-done.2
  80.4 0.9 copy.80
  81.2 4.5 %all-to-all-start.5 = ((f32[64,4,256]{2,1,0:T(4,128)}), f32[64,4,256]{2,1,0:T(4,128)S(1)}, u32[]{:S(2)}, u32[]{:S(2)}) async-start(f32[64,4,256]{2,1,0:T(4,128)} %copy.80), calls=%async_computation.5 | async-start | bytes 524288 | tf_op jit(solution)/shard_map/all_to_all | solution.py:47
  86.4 0.9 copy.77
  87.2 12.5 %all-to-all-done.5 = f32[64,4,256]{2,1,0:T(4,128)S(1)} async-done(((f32[64,4,256]{2,1,0:T(4,128)}), f32[64,4,256]{2,1,0:T(4,128)S(1)}, u32[]{:S(2)}, u32[]{:S(2)}) %all-to-all-start.5) | async-done | bytes 262176 | tf_op jit(solution)/shard_map/all_to_all | solution.py:47
  99.8 4.7 %all-to-all-start.2 = ((f32[64,4,256]{2,1,0:T(4,128)}), f32[64,4,256]{2,1,0:T(4,128)S(1)}, u32[]{:S(2)}, u32[]{:S(2)}) async-start(f32[64,4,256]{2,1,0:T(4,128)} %copy.77), calls=%async_computation.2 | async-start | bytes 524288 | tf_op jit(solution)/shard_map/all_to_all | solution.py:47
  105.1 0.9 copy.79
  106.0 12.5 %all-to-all-done.2 = f32[64,4,256]{2,1,0:T(4,128)S(1)} async-done(((f32[64,4,256]{2,1,0:T(4,128)}), f32[64,4,256]{2,1,0:T(4,128)S(1)}, u32[]{:S(2)}, u32[]{:S(2)}) %all-to-all-start.2) | async-done | bytes 262176 | tf_op jit(solution)/shard_map/all_to_all | solution.py:47
  118.5 4.5 %all-to-all-start.4 = ((f32[64,4,256]{2,1,0:T(4,128)}), f32[64,4,256]{2,1,0:T(4,128)S(1)}, u32[]{:S(2)}, u32[]{:S(2)}) async-start(f32[64,4,256]{2,1,0:T(4,128)} %copy.79), calls=%async_computation.4 | async-start | bytes 524288 | tf_op jit(solution)/shard_map/all_to_all | solution.py:47
  123.1 0.8 copy.63
  124.1 12.9 %all-to-all-done.4 = f32[64,4,256]{2,1,0:T(4,128)S(1)} async-done(((f32[64,4,256]{2,1,0:T(4,128)}), f32[64,4,256]{2,1,0:T(4,128)S(1)}, u32[]{:S(2)}, u32[]{:S(2)}) %all-to-all-start.4) | async-done | bytes 262176 | tf_op jit(solution)/shard_map/all_to_all | solution.py:47
  137.4 0.8 copy.60
  138.2 200.7 %psum.7 = f32[256]{0:T(256)S(1)} all-reduce(f32[256]{0:T(256)S(1)} %get-tuple-element.36), channel_id=1, replica_groups=mesh['ctx'=64,'tp'=4] {'ctx'}, use_global_device_ids=true, to_apply=%region_1.0 | all-reduce | flops 256 | bytes 2048 | tf_op jit(solution)/shard_map/psum | solution.py:72
  339.5 0.8 copy.59
  340.2 0.8 copy.61
  341.0 0.8 copy.62
  (55 shorter events, 9.4 us)
Async XLA Ops:
  0.6 1.1 copy-start.8
  2.6 14.0 %copy-start.9 = (bf16[256,256]{1,0:T(8,128)(2,1)S(1)}, bf16[256,256]{1,0:T(8,128)(2,1)}, u32[]{:S(2)}) copy-start(bf16[256,256]{1,0:T(8,128)(2,1)} %param.13) | copy-start | bytes 393220
  2.6 30.7 %all-to-all-start.3 = ((f32[64,4,256]{2,1,0:T(4,128)}), f32[64,4,256]{2,1,0:T(4,128)S(1)}, u32[]{:S(2)}, u32[]{:S(2)}) async-start(f32[64,4,256]{2,1,0:T(4,128)} %reshape.78), calls=%async_computation.3 | async-start | bytes 524288 | tf_op jit(solution)/shard_map/all_to_all | solution.py:42
  16.7 0.9 copy-start.10
  18.5 19.4 %copy-start.6 = (f32[256,256]{1,0:T(8,128)S(1)}, f32[256,256]{1,0:T(8,128)}, u32[]{:S(2)}) copy-start(f32[256,256]{1,0:T(8,128)} %param.15) | copy-start | bytes 786436
  33.4 19.6 %all-to-all-start = ((f32[64,4,256]{2,1,0:T(4,128)}), f32[64,4,256]{2,1,0:T(4,128)S(1)}, u32[]{:S(2)}, u32[]{:S(2)}) async-start(f32[64,4,256]{2,1,0:T(4,128)} %reshape.69), calls=%async_computation | async-start | bytes 524288 | tf_op jit(solution)/shard_map/all_to_all | solution.py:42
  53.0 18.6 %all-to-all-start.1 = ((f32[64,4,256]{2,1,0:T(4,128)}), f32[64,4,256]{2,1,0:T(4,128)S(1)}, u32[]{:S(2)}, u32[]{:S(2)}) async-start(f32[64,4,256]{2,1,0:T(4,128)} %reshape.72), calls=%async_computation.1 | async-start | bytes 524288 | tf_op jit(solution)/shard_map/all_to_all | solution.py:42
  58.0 0.9 copy-start.3
  71.9 0.9 copy-start.7
  72.8 0.8 copy-start.4
  72.8 0.9 copy-start.5
  73.7 0.9 copy-start.1
  76.6 1.0 copy-start
  78.8 0.9 copy-start.2
  81.2 18.5 %all-to-all-start.5 = ((f32[64,4,256]{2,1,0:T(4,128)}), f32[64,4,256]{2,1,0:T(4,128)S(1)}, u32[]{:S(2)}, u32[]{:S(2)}) async-start(f32[64,4,256]{2,1,0:T(4,128)} %copy.80), calls=%async_computation.5 | async-start | bytes 524288 | tf_op jit(solution)/shard_map/all_to_all | solution.py:47
  99.8 18.7 %all-to-all-start.2 = ((f32[64,4,256]{2,1,0:T(4,128)}), f32[64,4,256]{2,1,0:T(4,128)S(1)}, u32[]{:S(2)}, u32[]{:S(2)}) async-start(f32[64,4,256]{2,1,0:T(4,128)} %copy.77), calls=%async_computation.2 | async-start | bytes 524288 | tf_op jit(solution)/shard_map/all_to_all | solution.py:47
  118.5 18.5 %all-to-all-start.4 = ((f32[64,4,256]{2,1,0:T(4,128)}), f32[64,4,256]{2,1,0:T(4,128)S(1)}, u32[]{:S(2)}, u32[]{:S(2)}) async-start(f32[64,4,256]{2,1,0:T(4,128)} %copy.79), calls=%async_computation.4 | async-start | bytes 524288 | tf_op jit(solution)/shard_map/all_to_all | solution.py:47
  124.1 13.0 %copy-start.11 = (f32[256]{0:T(256)S(1)}, f32[256]{0:T(256)}, u32[]{:S(2)}) copy-start(f32[256]{0:T(256)} %param.16) | copy-start | bytes 3076

commit v2 on v1

v2 whole, which is shorter than its diff:
```python
import math

import jax
import jax.numpy as jnp
import numpy as np
from jax import lax
from jax.experimental import pallas as pl
from jax.experimental.pallas import tpu as pltpu
from jax.sharding import PartitionSpec as P

MESH = pl.DeviceIdType.MESH
F32 = jnp.float32
BF16 = jnp.bfloat16
HALF = 128
PLANE = 32
TILE = 8
BLOCK = PLANE * TILE
ROWS = 2 * BLOCK


def tables():
    half, z, source = np.meshgrid(np.arange(2), np.arange(2), np.arange(PLANE), indexing="ij")
    block = (source // 2) * 4 + z * 2 + source % 2
    n1 = (block * 2 + half).reshape(-1)
    k1 = np.arange(HALF) + 0.5
    n2 = np.arange(HALF)
    period = 2 * HALF * HALF
    first = 2 * np.pi * np.outer(k1, n1) / (2 * HALF)
    twist = 2 * np.pi * np.outer(k1, n2) / period
    second = 2 * np.pi * np.outer(n2, np.arange(HALF)) / HALF
    c2, s2 = np.cos(second), np.sin(second)
    f1 = np.concatenate([np.cos(first), -np.sin(first)], 0)
    f2 = np.block([[c2, -s2], [s2, c2]])
    g2 = np.block([[c2, s2], [-s2, c2]])
    g1 = np.concatenate([np.cos(first).T, -np.sin(first).T], 1) * (2 / period)
    return [t.astype(np.float32) for t in (f1, f2, g1, g2, np.cos(twist), -np.sin(twist))]


def split(x):
    high = x.astype(BF16)
    return high, (x - high.astype(F32)).astype(BF16)


def dot(a, b):
    return jnp.dot(a, b, preferred_element_type=F32)


def dot3(a, b):
    return dot(a[0], b[0]) + (dot(a[0], b[1]) + dot(a[1], b[0]))


def kernel(
    q_in, k_in, v_in, taps_in, skip_in, cot_in,
    f1_in, f2_in, g1_in, g2_in, tr_in, ti_in,
    gated_out, gq_out, gk_out, gv_out, gt_out, gs_out,
    q, k, v, taps, skip, cot,
    f1, f2, g1, g2, tr, ti,
    gated, gq, gk, gv, gt, gs,
    sa1, sa2, sa3, sb1, sb2, sb3,
    ea1, ea2, ea3, eb1, eb2, eb3,
    ra1, ra2, ra3, rb1, rb2, rb3,
    spec_u, spec_h, spec_g,
    skip_send, skip_recv, f1h, f1l, f2h, f2l, g1h, g1l, g2h, g2l,
    load_sem, store_sem, z_send, z_recv, own_send, fwd_send, plane_recv, mid_recv, sk_send, sk_recv,
):
    ctx = lax.axis_index("ctx")
    core, mz, yx = ctx % 2, (ctx // 2) % 2, ctx // 4
    oz = 1 - mz
    me = yx * 2 + core
    yblk, m8 = me // 8, me % 8
    x, y = yx % 4, yx // 4

    def plane_device(p):
        return {"ctx": (p // 2) * 4 + mz * 2 + p % 2}

    def peer(t):
        return ((yblk + t // 8) % 4) * 8 + (m8 + t % 8) % 8

    z_device = {"ctx": yx * 4 + oz * 2 + core}

    def rows(start, count):
        return pl.ds(pl.multiple_of(start, TILE), count)

    barrier = pltpu.get_barrier_semaphore()

    def greet(t, carry):
        pl.semaphore_signal(barrier, inc=1, device_id=plane_device(peer(t)), device_id_type=MESH)
        return carry

    sources = (k_in, v_in, taps_in, q_in, cot_in, f1_in, f2_in, g2_in, g1_in, tr_in, ti_in, skip_in)
    targets = (k, v, taps, q, cot, f1, f2, g2, g1, tr, ti, skip)
    loads = [pltpu.make_async_copy(s, t, load_sem.at[i]) for i, (s, t) in enumerate(zip(sources, targets))]
    for load in loads:
        load.start()
    pl.semaphore_signal(barrier, inc=1, device_id=z_device, device_id_type=MESH)
    lax.fori_loop(1, PLANE, greet, 0)

    def wait_rows(ref, count, sem):
        pltpu.make_async_copy(ref.at[pl.ds(0, count)], ref.at[pl.ds(0, count)], sem).wait()

    def plane_sends(src, src_base, dst, dst_row, send_sem, recv_sem, lo=1, hi=PLANE):
        def body(t, carry):
            p = peer(t)
            pltpu.make_async_remote_copy(
                src_ref=src.at[rows(src_base + p * TILE, TILE)],
                dst_ref=dst.at[rows(dst_row, TILE)],
                send_sem=send_sem,
                recv_sem=recv_sem,
                device_id=plane_device(p),
                device_id_type=MESH,
            ).start()
            return carry

        if lo == 1:
            dst[rows(dst_row, TILE), :] = src[rows(src_base + me * TILE, TILE), :]
        lax.fori_loop(lo, hi, body, 0)

    CHUNKS = 4
    CROWS = BLOCK // CHUNKS

    def z_copy(s, e, i, j):
        start = ((yblk + j) % CHUNKS) * CROWS
        return pltpu.make_async_remote_copy(
            src_ref=s.at[rows(oz * BLOCK + start, CROWS)],
            dst_ref=e.at[rows(start, CROWS)],
            send_sem=z_send.at[i, j],
            recv_sem=z_recv.at[i, j],
            device_id=z_device,
            device_id_type=MESH,
        )

    def z_first(i, s, e, r):
        for j in range(CHUNKS):
            z_copy(s, e, i, j).start()
        plane_sends(s, mz * BLOCK, r, (mz * PLANE + me) * TILE, own_send.at[i], plane_recv.at[i])

    def forward(i, s, e, r):
        for j in range(CHUNKS):
            z_copy(s, e, i, j).wait_recv()
            plane_sends(e, 0, r, (oz * PLANE + me) * TILE, fwd_send.at[i], plane_recv.at[i],
                        max(1, 8 * j), 8 * (j + 1))

    def arrived(i, r):
        wait_rows(r, 2 * (BLOCK - TILE), plane_recv.at[i])

    def drain(i, s, e, r):
        for j in range(CHUNKS):
            z_copy(s, e, i, j).wait_send()
        wait_rows(r, BLOCK - TILE, own_send.at[i])
        wait_rows(r, BLOCK - TILE, fwd_send.at[i])

    def put(s, fs, values, h):
        flipped = values.T
        for c in range(2):
            s[pl.ds(fs * 4 + c * 2 + h, 64, stride=TILE), :] = flipped[c * 64 : (c + 1) * 64]

    def piece(ref, h, pair):
        return ref[h * HALF : (h + 1) * HALF, pair * HALF : (pair + 1) * HALF].astype(F32)

    def put_inputs(s, pair):
        for h in range(2):
            put(s, 0, piece(k, h, pair) * piece(v, h, pair), h)
            put(s, 1, piece(taps, h, pair), h)

    def put_grad(s):
        for pair in range(2):
            for h in range(2):
                put(s, pair, piece(q, h, pair) * piece(cot, h, pair), h)

    def forward_pair(r, fs, spec, pair):
        series = []
        for c in range(2):
            parts = [r[pl.ds(z * BLOCK + fs * 4 + c * 2 + h, PLANE, stride=TILE), :] for h in range(2) for z in range(2)]
            series.append(jnp.concatenate(parts, 0))
        a = dot3((f1h[...], f1l[...]), split(jnp.concatenate(series, 1)))
        tc, ts = tr[...], ti[...]
        turned = []
        for c in range(2):
            ar, ai = a[:HALF, c * HALF : (c + 1) * HALF], a[HALF:, c * HALF : (c + 1) * HALF]
            turned.append(jnp.concatenate([ar * tc - ai * ts, ar * ts + ai * tc], 1))
        b = dot3(split(jnp.concatenate(turned, 0)), (f2h[...], f2l[...]))
        for c in range(2):
            spec[pair * 2 + c] = b[c * HALF : (c + 1) * HALF]

    def inverse_pair(a, b, pair, conj, s, fs):
        prods = []
        for c in range(2):
            l, m = a[pair * 2 + c], b[pair * 2 + c]
            lr, li, mr, mi = l[:, :HALF], l[:, HALF:], m[:, :HALF], m[:, HALF:]
            if conj:
                prods.append(jnp.concatenate([lr * mr + li * mi, lr * mi - li * mr], 1))
            else:
                prods.append(jnp.concatenate([lr * mr - li * mi, lr * mi + li * mr], 1))
        d = dot3(split(jnp.concatenate(prods, 0)), (g2h[...], g2l[...]))
        tc, ts = tr[...], ti[...]
        turned = []
        for c in range(2):
            dr, di = d[c * HALF : (c + 1) * HALF, :HALF], d[c * HALF : (c + 1) * HALF, HALF:]
            turned.append(jnp.concatenate([dr * tc + di * ts, di * tc - dr * ts], 0))
        out = dot3((g1h[...], g1l[...]), split(jnp.concatenate(turned, 1)))
        for c in range(2):
            for h in range(2):
                for z in range(2):
                    start = (h * 2 + z) * PLANE
                    s[pl.ds(z * BLOCK + fs * 4 + c * 2 + h, PLANE, stride=TILE), :] = out[
                        start : start + PLANE, c * HALF : (c + 1) * HALF
                    ]

    def take(r, fs, h):
        parts = [r[pl.ds(fs * 4 + c * 2 + h, 2 * PLANE, stride=TILE), :] for c in range(2)]
        return jnp.concatenate(parts, 0).T

    partners = (
        {"ctx": yx * 4 + mz * 2 + 1 - core},
        {"ctx": (y * 4 + x + 1 - 2 * (x % 2)) * 4 + mz * 2 + core},
        {"ctx": (y * 4 + (x + 2) % 4) * 4 + mz * 2 + core},
        {"ctx": ((y + 1 - 2 * (y % 2)) * 4 + x) * 4 + mz * 2 + core},
        {"ctx": (((y + 2) % 4) * 4 + x) * 4 + mz * 2 + core},
        z_device,
    )

    def skip_copy(i):
        return pltpu.make_async_remote_copy(
            src_ref=skip_send.at[i], dst_ref=skip_recv.at[i], send_sem=sk_send.at[i], recv_sem=sk_recv.at[i],
            device_id=partners[i], device_id_type=MESH,
        )

    def skip_step(i):
        skip_copy(i).wait_recv()
        total = skip_send[i] + skip_recv[i]
        if i + 1 < len(partners):
            skip_send[i + 1] = total
            skip_copy(i + 1).start()
        else:
            gs[...] = jnp.sum(total, axis=0, keepdims=True) * (1.0 / HALF)

    for i in range(3):
        loads[i].wait()
    put_inputs(sa1, 0)
    pl.semaphore_wait(barrier, PLANE)
    z_first(0, sa1, ea1, ra1)
    for i in range(3, 5):
        loads[i].wait()
    put_grad(sa2)
    z_first(1, sa2, ea2, ra2)
    put_inputs(sa3, 1)
    z_first(2, sa3, ea3, ra3)
    total = jnp.zeros((TILE, 2 * HALF), F32)
    for i in range(4):
        part = slice(i * 64, (i + 1) * 64)
        prod = (k[part, :].astype(F32) * v[part, :].astype(F32)) * (q[part, :].astype(F32) * cot[part, :].astype(F32))
        total = total + jnp.sum(prod.reshape(8, TILE, 2 * HALF), axis=0)
    skip_send[0] = total
    skip_copy(0).start()
    for i in range(5, len(loads)):
        loads[i].wait()
    for table, high, low in ((f1, f1h, f1l), (f2, f2h, f2l), (g2, g2h, g2l), (g1, g1h, g1l)):
        high[...], low[...] = split(table[...])

    forward(0, sa1, ea1, ra1)
    skip_step(0)
    arrived(0, ra1)
    forward_pair(ra1, 0, spec_u, 0)
    forward_pair(ra1, 1, spec_h, 0)
    inverse_pair(spec_u, spec_h, 0, False, sb2, 0)
    forward(1, sa2, ea2, ra2)
    skip_step(1)
    arrived(1, ra2)
    forward_pair(ra2, 0, spec_g, 0)
    inverse_pair(spec_h, spec_g, 0, True, sb1, 0)
    inverse_pair(spec_u, spec_g, 0, True, sb1, 1)
    z_first(3, sb1, eb1, rb1)
    forward_pair(ra2, 1, spec_g, 1)
    forward(2, sa3, ea3, ra3)
    skip_step(2)
    arrived(2, ra3)
    forward_pair(ra3, 0, spec_u, 1)
    forward_pair(ra3, 1, spec_h, 1)
    inverse_pair(spec_u, spec_h, 1, False, sb2, 1)
    z_first(4, sb2, eb2, rb2)
    skip_step(3)
    inverse_pair(spec_h, spec_g, 1, True, sb3, 0)
    inverse_pair(spec_u, spec_g, 1, True, sb3, 1)
    plane_sends(sb3, oz * BLOCK, eb3, me * TILE, fwd_send.at[5], mid_recv)
    plane_sends(sb3, mz * BLOCK, rb3, (mz * PLANE + me) * TILE, own_send.at[5], plane_recv.at[5])
    skip_step(4)
    forward(3, sb1, eb1, rb1)
    wait_rows(eb3, BLOCK - TILE, mid_recv)
    last = pltpu.make_async_remote_copy(
        src_ref=eb3, dst_ref=rb3.at[rows(mz * BLOCK, BLOCK)], send_sem=z_send.at[5, 0], recv_sem=z_recv.at[5, 0],
        device_id=z_device, device_id_type=MESH,
    )
    last.start()
    skip_step(5)

    def finish_grad(r, pair):
        cols = slice(pair * HALF, (pair + 1) * HALF)
        bias = skip[:, cols]
        for h in range(2):
            at = slice(h * HALF, (h + 1) * HALF)
            grad = take(r, 0, h) + bias * (piece(q, h, pair) * piece(cot, h, pair))
            gk[at, cols] = (grad * piece(v, h, pair)).astype(BF16)
            gv[at, cols] = (grad * piece(k, h, pair)).astype(BF16)
            gt[at, cols] = take(r, 1, h) * (1.0 / HALF)

    def finish_mixed(r):
        for pair in range(2):
            cols = slice(pair * HALF, (pair + 1) * HALF)
            bias = skip[:, cols]
            for h in range(2):
                at = slice(h * HALF, (h + 1) * HALF)
                mixed = take(r, pair, h) + bias * (piece(k, h, pair) * piece(v, h, pair))
                gated[at, cols] = (piece(q, h, pair) * mixed).astype(BF16)
                gq[at, cols] = (piece(cot, h, pair) * mixed).astype(BF16)

    stores = [
        pltpu.make_async_copy(s, t, store_sem.at[i])
        for i, (s, t) in enumerate(
            zip((gated, gq, gs, gk, gv, gt), (gated_out, gq_out, gs_out, gk_out, gv_out, gt_out))
        )
    ]
    arrived(3, rb1)
    finish_grad(rb1, 0)
    forward(4, sb2, eb2, rb2)
    arrived(4, rb2)
    finish_mixed(rb2)
    for store in stores[:3]:
        store.start()
    wait_rows(rb3, BLOCK - TILE, plane_recv.at[5])
    for i, (s, e, r) in enumerate(
        ((sa1, ea1, ra1), (sa2, ea2, ra2), (sa3, ea3, ra3), (sb1, eb1, rb1), (sb2, eb2, rb2))
    ):
        drain(i, s, e, r)
    wait_rows(rb3, BLOCK - TILE, own_send.at[5])
    wait_rows(rb3, BLOCK - TILE, fwd_send.at[5])
    for i in range(len(partners)):
        skip_copy(i).wait_send()
    last.wait()
    finish_grad(rb3, 1)
    for store in stores[3:]:
        store.start()
    for store in stores:
        store.wait()


def shards(query_proj, key_proj, value_proj, filter_taps, skip_bias, cotangent):
    consts = [jnp.asarray(t) for t in tables()]
    shape = query_proj.shape
    args = (query_proj, key_proj, value_proj, filter_taps, skip_bias.reshape(1, -1), cotangent, *consts)
    outs = [jax.ShapeDtypeStruct(shape, BF16)] * 4 + [
        jax.ShapeDtypeStruct(shape, F32),
        jax.ShapeDtypeStruct((1, shape[1]), F32),
    ]
    anywhere = pl.BlockSpec(memory_space=pl.ANY)
    vmem = lambda *s: pltpu.VMEM(s, F32)
    dma = pltpu.SemaphoreType.DMA
    results = pl.pallas_call(
        kernel,
        out_shape=outs,
        in_specs=[anywhere] * len(args),
        out_specs=[anywhere] * len(outs),
        scratch_shapes=[pltpu.VMEM(a.shape, a.dtype) for a in args]
        + [pltpu.VMEM(o.shape, o.dtype) for o in outs]
        + [vmem(ROWS, HALF)] * 6
        + [vmem(BLOCK, HALF)] * 6
        + [vmem(ROWS, HALF)] * 6
        + [vmem(4, HALF, 2 * HALF)] * 3
        + [vmem(6, TILE, 2 * HALF)] * 2
        + [pltpu.VMEM(s, BF16) for s in ((256, 128), (256, 256), (128, 256), (256, 256)) for _ in range(2)]
        + [dma((12,)), dma((6,)), dma((6, 4)), dma((6, 4)), dma((6,)), dma((6,)), dma((6,)), dma, dma((6,)), dma((6,))],
        compiler_params=pltpu.CompilerParams(
            collective_id=0, has_side_effects=True, vmem_limit_bytes=56 * 1024 * 1024
        ),
        name="long_conv",
    )(*args)
    gated, grad_query, grad_key, grad_value, grad_taps, grad_skip = results
    return gated, grad_query, grad_key, grad_value, grad_taps, grad_skip.reshape(-1)


def solution(mesh):
    s = P("ctx", "tp")
    return jax.shard_map(
        shards, mesh=mesh, in_specs=(s, s, s, s, P("tp"), s), out_specs=(s, s, s, s, s, P("tp")), check_vma=False
    )
```

time: 344 us -> 68 us (0.20)
  the two profiles are of different devices: /device:TPU:33 before, /device:TPU:65 now
where the time goes in v2:
time: 68 us; the launch traced here: 67.9 us
  Pallas kernels  62.1 us (91%)
  local copies, waits for them, and re-layouts  5.14 us (8%)
    pallas_call x1, Pallas kernels, shards(): pl.pallas_call(kernel, out_shape=outs, in_specs=[anywhere] * len(args), o...  62.1 us
    unnamed x16, local copies, waits for them, and re-layouts  5.14 us

profile of v2, /device:TPU:65, one launch (start us, length us, event | category | flops | bytes accessed | tf_op | source)
XLA Modules:
  0.0 67.9 jit_solution(75382943429521944)
XLA Ops:
  0.6 62.1 %long_conv.1 = (bf16[256,256]{1,0:T(8,128)(2,1)}, bf16[256,256]{1,0:T(8,128)(2,1)}, bf16[256,256]{1,0:T(8,128)(2,1)}, bf16[256,256]{1,0:T(8,128)(2,1)}, f32[256,256]{1,0:T(8,128)}, /*index=5*/f32[1,256]{1,0:T(1,128)}) custom-call(bf16[256,256]{1,0:T(8,128)(2,1)} %q_in.1, bf16[256,256]{1,0:T(8,128)(2,1)} %k_in.1, bf16[256,256]{1,0:T(8,128)(2,1)} %v_in.1, ...), custom_call_target="tpu_custom_call" | custom-call | tf_op jit(solution)/shard_map/long_conv/pallas_call | solution.py:357
  62.7 0.0 copy-start.3
  62.7 1.6 %copy.24 = bf16[256,256]{1,0:T(8,128)(2,1)} copy(bf16[256,256]{1,0:T(8,128)(2,1)} %get-tuple-element.24) | data formatting | bytes 262144
  64.3 0.0 copy-done.3
  64.3 0.0 copy-start.2
  64.3 0.0 copy-start.1
  64.3 0.7 copy.25
  65.0 0.3 copy-done.2
  65.3 0.0 copy-start
  65.3 0.7 copy.26
  65.9 0.0 copy-done.1
  65.9 0.7 copy.27
  66.6 0.0 copy-done
  66.6 0.0 copy-start.4
  66.6 0.7 %copy.28 = f32[256,256]{1,0:T(8,128)} copy(f32[256,256]{1,0:T(8,128)S(1)} %copy-done) | data formatting | bytes 524288
  67.3 0.0 copy-done.4
  67.3 0.6 copy.29
Async XLA Ops:
  62.7 1.6 %copy-start.3 = (bf16[256,256]{1,0:T(8,128)(2,1)S(1)}, bf16[256,256]{1,0:T(8,128)(2,1)}, u32[]{:S(2)}) copy-start(bf16[256,256]{1,0:T(8,128)(2,1)} %get-tuple-element.25) | copy-start | bytes 393220
  64.3 1.0 %copy-start.2 = (bf16[256,256]{1,0:T(8,128)(2,1)S(1)}, bf16[256,256]{1,0:T(8,128)(2,1)}, u32[]{:S(2)}) copy-start(bf16[256,256]{1,0:T(8,128)(2,1)} %get-tuple-element.26) | copy-start | bytes 393220
  64.3 1.6 %copy-start.1 = (bf16[256,256]{1,0:T(8,128)(2,1)S(1)}, bf16[256,256]{1,0:T(8,128)(2,1)}, u32[]{:S(2)}) copy-start(bf16[256,256]{1,0:T(8,128)(2,1)} %get-tuple-element.27) | copy-start | bytes 393220
  65.3 1.3 %copy-start = (f32[256,256]{1,0:T(8,128)S(1)}, f32[256,256]{1,0:T(8,128)}, u32[]{:S(2)}) copy-start(f32[256,256]{1,0:T(8,128)} %get-tuple-element.28) | copy-start | bytes 786436
  66.6 0.7 %copy-start.4 = (f32[1,256]{1,0:T(1,128)S(1)}, f32[1,256]{1,0:T(1,128)}, u32[]{:S(2)}) copy-start(f32[1,256]{1,0:T(1,128)} %get-tuple-element.17) | copy-start | bytes 3076

commit v3 on v2

v3 whole, which is shorter than its diff:
```python
import math

import jax
import jax.numpy as jnp
import numpy as np
from jax import lax
from jax.experimental import pallas as pl
from jax.experimental.pallas import tpu as pltpu
from jax.sharding import PartitionSpec as P

MESH = pl.DeviceIdType.MESH
F32 = jnp.float32
BF16 = jnp.bfloat16
HALF = 128
PLANE = 32
TILE = 8
OWNERS = 2 * PLANE
UNIT = 6
MESSAGE = 4 * UNIT
ROWS = OWNERS * MESSAGE


def tables():
    half, z, source = np.meshgrid(np.arange(2), np.arange(2), np.arange(PLANE), indexing="ij")
    block = (source // 2) * 4 + z * 2 + source % 2
    n1 = (block * 2 + half).reshape(-1)
    k1 = np.arange(HALF) + 0.5
    n2 = np.arange(HALF)
    period = 2 * HALF * HALF
    first = 2 * np.pi * np.outer(k1, n1) / (2 * HALF)
    twist = 2 * np.pi * np.outer(k1, n2) / period
    second = 2 * np.pi * np.outer(n2, np.arange(HALF)) / HALF
    c2, s2 = np.cos(second), np.sin(second)
    f1 = np.concatenate([np.cos(first), -np.sin(first)], 0)
    f2 = np.block([[c2, -s2], [s2, c2]])
    g2 = np.block([[c2, s2], [-s2, c2]])
    g1 = np.concatenate([np.cos(first).T, -np.sin(first).T], 1) * (2 / period)
    return [t.astype(np.float32) for t in (f1, f2, g1, g2, np.cos(twist), -np.sin(twist))]


def split(x):
    high = x.astype(BF16)
    return high, (x - high.astype(F32)).astype(BF16)


def dot(a, b):
    return jnp.dot(a, b, preferred_element_type=F32)


def dot3(a, b):
    return dot(a[0], b[0]) + (dot(a[0], b[1]) + dot(a[1], b[0]))


def kernel(
    q_in, k_in, v_in, taps_in, skip_in, cot_in,
    f1_in, f2_in, g1_in, g2_in, tr_in, ti_in,
    gated_out, gq_out, gk_out, gv_out, gt_out, gs_out,
    q, k, v, taps, skip, cot,
    f1, f2, g1, g2, tr, ti,
    gated, gq, gk, gv, gt, gs,
    sa, sb, ra, rb,
    skip_send, skip_recv, f1h, f1l, f2h, f2l, g1h, g1l, g2h, g2l,
    load_sem, store_sem, send_sem, recv_sem, sk_send, sk_recv,
):
    ctx = lax.axis_index("ctx")
    core, mz, yx = ctx % 2, (ctx // 2) % 2, ctx // 4
    oz = 1 - mz
    me = yx * 2 + core
    yblk, m8 = me // 8, me % 8
    x, y = yx % 4, yx // 4

    def device(z, p):
        return {"ctx": (p // 2) * 4 + z * 2 + p % 2}

    def peer(dy, t):
        a = 2 + 3 * (t // 2)
        dx = jnp.where(t >= 4, 3 - a % 4, a % 4)
        return ((y + dy) % 4 * 4 + (x + dx) % 4) * 2 + (core + 1 - t % 2) % 2

    def to_others(action):
        for z in (oz, mz):
            for dy in (2, 1, 3, 0):

                def body(t, carry, z=z, dy=dy):
                    action(z, peer(dy, t))
                    return carry

                lax.fori_loop(0, 7 if z is mz and dy == 0 else 8, body, 0)

    z_device = {"ctx": yx * 4 + oz * 2 + core}

    def part(owner, c):
        return pl.ds(pl.multiple_of(owner * MESSAGE, TILE) + c * UNIT, UNIT)

    barrier = pltpu.get_barrier_semaphore()

    def greet(z, p):
        pl.semaphore_signal(barrier, inc=1, device_id=device(z, p), device_id_type=MESH)

    sources = (k_in, v_in, taps_in, q_in, cot_in, f1_in, f2_in, g2_in, g1_in, tr_in, ti_in, skip_in)
    targets = (k, v, taps, q, cot, f1, f2, g2, g1, tr, ti, skip)
    loads = [pltpu.make_async_copy(s, t, load_sem.at[i]) for i, (s, t) in enumerate(zip(sources, targets))]
    to_others(greet)
    for load in loads:
        load.start()

    def wait_rows(ref, count, sem):
        pltpu.make_async_copy(ref.at[pl.ds(0, count)], ref.at[pl.ds(0, count)], sem).wait()

    def send(i, c, src, dst):
        mine = part(mz * PLANE + me, c)

        def one(z, p):
            pltpu.make_async_remote_copy(
                src_ref=src.at[part(z * PLANE + p, c)],
                dst_ref=dst.at[mine],
                send_sem=send_sem.at[i],
                recv_sem=recv_sem.at[i],
                device_id=device(z, p),
                device_id_type=MESH,
            ).start()

        to_others(one)
        dst[mine, :] = src[mine, :]

    def arrived(i, r):
        wait_rows(r, (OWNERS - 1) * UNIT, recv_sem.at[i])

    def put(s, pair, field, values, h):
        flipped = values.T
        for c in range(2):
            s[pl.ds((pair * 2 + c) * UNIT + field * 2 + h, OWNERS, stride=MESSAGE), :] = flipped[
                c * OWNERS : (c + 1) * OWNERS
            ]

    def piece(ref, h, pair):
        return ref[h * HALF : (h + 1) * HALF, pair * HALF : (pair + 1) * HALF].astype(F32)

    def lay_out(s, pair):
        for h in range(2):
            put(s, pair, 0, piece(k, h, pair) * piece(v, h, pair), h)
            put(s, pair, 1, piece(taps, h, pair), h)
            put(s, pair, 2, piece(q, h, pair) * piece(cot, h, pair), h)

    def series_rows(c, field, h, z):
        return pl.ds(z * PLANE * MESSAGE + c * UNIT + field * 2 + h, PLANE, stride=MESSAGE)

    def transform(c):
        series = []
        for field in range(3):
            parts = [ra[series_rows(c, field, h, z), :] for h in range(2) for z in range(2)]
            series.append(jnp.concatenate(parts, 0))
        a = dot3((f1h[...], f1l[...]), split(jnp.concatenate(series, 1)))
        tc, ts = tr[...], ti[...]
        turned = []
        for field in range(3):
            cols = slice(field * HALF, (field + 1) * HALF)
            ar, ai = a[:HALF, cols], a[HALF:, cols]
            turned.append(jnp.concatenate([ar * tc - ai * ts, ar * ts + ai * tc], 1))
        b = dot3(split(jnp.concatenate(turned, 0)), (f2h[...], f2l[...]))
        (ur, ui), (hr, hi), (gr, gi) = [
            (b[f * HALF : (f + 1) * HALF, :HALF], b[f * HALF : (f + 1) * HALF, HALF:]) for f in range(3)
        ]
        prods = jnp.concatenate(
            [
                jnp.concatenate([ur * hr - ui * hi, ur * hi + ui * hr], 1),
                jnp.concatenate([hr * gr + hi * gi, hr * gi - hi * gr], 1),
                jnp.concatenate([ur * gr + ui * gi, ur * gi - ui * gr], 1),
            ],
            0,
        )
        d = dot3(split(prods), (g2h[...], g2l[...]))
        turned = []
        for field in range(3):
            at = slice(field * HALF, (field + 1) * HALF)
            dr, di = d[at, :HALF], d[at, HALF:]
            turned.append(jnp.concatenate([dr * tc + di * ts, di * tc - dr * ts], 0))
        out = dot3((g1h[...], g1l[...]), split(jnp.concatenate(turned, 1)))
        for field in range(3):
            for h in range(2):
                for z in range(2):
                    start = (h * 2 + z) * PLANE
                    sb[series_rows(c, field, h, z), :] = out[
                        start : start + PLANE, field * HALF : (field + 1) * HALF
                    ]

    def take(pair, field, h):
        parts = [
            rb[pl.ds((pair * 2 + c) * UNIT + field * 2 + h, OWNERS, stride=MESSAGE), :] for c in range(2)
        ]
        return jnp.concatenate(parts, 0).T

    partners = (
        {"ctx": yx * 4 + mz * 2 + 1 - core},
        {"ctx": (y * 4 + x + 1 - 2 * (x % 2)) * 4 + mz * 2 + core},
        {"ctx": (y * 4 + (x + 2) % 4) * 4 + mz * 2 + core},
        {"ctx": ((y + 1 - 2 * (y % 2)) * 4 + x) * 4 + mz * 2 + core},
        {"ctx": (((y + 2) % 4) * 4 + x) * 4 + mz * 2 + core},
        z_device,
    )

    def skip_copy(i):
        return pltpu.make_async_remote_copy(
            src_ref=skip_send.at[i], dst_ref=skip_recv.at[i], send_sem=sk_send.at[i], recv_sem=sk_recv.at[i],
            device_id=partners[i], device_id_type=MESH,
        )

    def skip_step(i):
        skip_copy(i).wait_recv()
        total = skip_send[i] + skip_recv[i]
        if i + 1 < len(partners):
            skip_send[i + 1] = total
            skip_copy(i + 1).start()
        else:
            gs[...] = jnp.sum(total, axis=0, keepdims=True) * (1.0 / HALF)

    for i in range(5):
        loads[i].wait()
    for pair in range(2):
        lay_out(sa, pair)
    pl.semaphore_wait(barrier, OWNERS - 1)
    for c in range(4):
        send(c, c, sa, ra)
    total = jnp.zeros((TILE, 2 * HALF), F32)
    for i in range(4):
        at = slice(i * 64, (i + 1) * 64)
        prod = (k[at, :].astype(F32) * v[at, :].astype(F32)) * (q[at, :].astype(F32) * cot[at, :].astype(F32))
        total = total + jnp.sum(prod.reshape(8, TILE, 2 * HALF), axis=0)
    skip_send[0] = total
    skip_copy(0).start()
    for i in range(5, len(loads)):
        loads[i].wait()
    for table, high, low in ((f1, f1h, f1l), (f2, f2h, f2l), (g2, g2h, g2l), (g1, g1h, g1l)):
        high[...], low[...] = split(table[...])
    skip_step(0)
    for c in range(4):
        arrived(c, ra)
        transform(c)
        send(4 + c, c, sb, rb)
        skip_step(c + 1)

    def finish(pair):
        cols = slice(pair * HALF, (pair + 1) * HALF)
        bias = skip[:, cols]
        for h in range(2):
            at = slice(h * HALF, (h + 1) * HALF)
            qp, kp, vp, cp = [piece(ref, h, pair) for ref in (q, k, v, cot)]
            mixed = take(pair, 0, h) + bias * (kp * vp)
            gated[at, cols] = (qp * mixed).astype(BF16)
            gq[at, cols] = (cp * mixed).astype(BF16)
            grad = take(pair, 1, h) + bias * (qp * cp)
            gk[at, cols] = (grad * vp).astype(BF16)
            gv[at, cols] = (grad * kp).astype(BF16)
            gt[at, cols] = take(pair, 2, h) * (1.0 / HALF)

    stores = [
        pltpu.make_async_copy(s, t, store_sem.at[i])
        for i, (s, t) in enumerate(
            zip((gated, gq, gs, gk, gv, gt), (gated_out, gq_out, gs_out, gk_out, gv_out, gt_out))
        )
    ]
    arrived(4, rb)
    arrived(5, rb)
    finish(0)
    skip_step(5)
    for i in range(8):
        wait_rows(ra, (OWNERS - 1) * UNIT, send_sem.at[i])
    for i in range(len(partners)):
        skip_copy(i).wait_send()
    arrived(6, rb)
    arrived(7, rb)
    finish(1)
    for store in stores:
        store.start()
    for store in stores:
        store.wait()


def hand_on(*refs):
    count = len(refs) // 3
    into, out = refs[-2:]
    reads = [pltpu.make_async_copy(refs[i], refs[2 * count + i], into.at[i]) for i in range(count)]
    writes = [pltpu.make_async_copy(refs[2 * count + i], refs[count + i], out.at[i]) for i in range(count)]
    for read in reads:
        read.start()
    for read, write in zip(reads, writes):
        read.wait()
        write.start()
    for write in writes:
        write.wait()


def shards(query_proj, key_proj, value_proj, filter_taps, skip_bias, cotangent):
    consts = [jnp.asarray(t) for t in tables()]
    shape = query_proj.shape
    args = (query_proj, key_proj, value_proj, filter_taps, skip_bias.reshape(1, -1), cotangent, *consts)
    outs = [jax.ShapeDtypeStruct(shape, BF16)] * 4 + [
        jax.ShapeDtypeStruct(shape, F32),
        jax.ShapeDtypeStruct((1, shape[1]), F32),
    ]
    anywhere = pl.BlockSpec(memory_space=pl.ANY)
    vmem = lambda *s: pltpu.VMEM(s, F32)
    dma = pltpu.SemaphoreType.DMA
    results = pl.pallas_call(
        kernel,
        out_shape=outs,
        in_specs=[anywhere] * len(args),
        out_specs=[anywhere] * len(outs),
        scratch_shapes=[pltpu.VMEM(a.shape, a.dtype) for a in args]
        + [pltpu.VMEM(o.shape, o.dtype) for o in outs]
        + [vmem(ROWS, HALF)] * 4
        + [vmem(6, TILE, 2 * HALF)] * 2
        + [pltpu.VMEM(s, BF16) for s in ((256, 128), (256, 256), (128, 256), (256, 256)) for _ in range(2)]
        + [dma((12,)), dma((6,)), dma((8,)), dma((8,)), dma((6,)), dma((6,))],
        compiler_params=pltpu.CompilerParams(
            collective_id=0, has_side_effects=True, vmem_limit_bytes=56 * 1024 * 1024
        ),
        name="long_conv",
    )(*args)
    gated, grad_query, grad_key, grad_value, grad_taps, grad_skip = pl.pallas_call(
        hand_on,
        out_shape=outs,
        in_specs=[anywhere] * len(outs),
        out_specs=[anywhere] * len(outs),
        scratch_shapes=[pltpu.VMEM(o.shape, o.dtype) for o in outs] + [dma((len(outs),))] * 2,
        compiler_params=pltpu.CompilerParams(vmem_limit_bytes=56 * 1024 * 1024),
        name="hand_on",
    )(*results)
    return gated, grad_query, grad_key, grad_value, grad_taps, grad_skip.reshape(-1)


def solution(mesh):
    s = P("ctx", "tp")
    return jax.shard_map(
        shards, mesh=mesh, in_specs=(s, s, s, s, P("tp"), s), out_specs=(s, s, s, s, s, P("tp")), check_vma=False
    )
```

time: 68 us -> 53.6 us (0.79)
  the two profiles are of different devices: /device:TPU:65 before, /device:TPU:33 now
where the time goes in v3:
time: 53.6 us; the launch traced here: 53.5 us
  Pallas kernels  52.9 us (99%)
  between operations  0.64 us (1%)
    pallas_call x1, Pallas kernels, shards(): pl.pallas_call(kernel, out_shape=outs, in_specs=[anywhere] * len(args), o...  50.8 us
    pallas_call x1, Pallas kernels, shards(): pl.pallas_call(hand_on, out_shape=outs, in_specs=[anywhere] * len(outs),...  2.02 us

profile of v3, /device:TPU:33, one launch (start us, length us, event | category | flops | bytes accessed | tf_op | source)
XLA Modules:
  0.0 53.5 jit_solution(12970644890028608028)
XLA Ops:
  0.6 50.8 %long_conv.1 = (bf16[256,256]{1,0:T(8,128)(2,1)}, bf16[256,256]{1,0:T(8,128)(2,1)}, bf16[256,256]{1,0:T(8,128)(2,1)}, bf16[256,256]{1,0:T(8,128)(2,1)}, f32[256,256]{1,0:T(8,128)}, /*index=5*/f32[1,256]{1,0:T(1,128)}) custom-call(bf16[256,256]{1,0:T(8,128)(2,1)} %q_in.1, bf16[256,256]{1,0:T(8,128)(2,1)} %k_in.1, bf16[256,256]{1,0:T(8,128)(2,1)} %v_in.1, ...), custom_call_target="tpu_custom_call" | custom-call | tf_op jit(solution)/shard_map/long_conv/pallas_call | solution.py:304
  51.5 2.0 %hand_on.1 = (bf16[256,256]{1,0:T(8,128)(2,1)}, bf16[256,256]{1,0:T(8,128)(2,1)}, bf16[256,256]{1,0:T(8,128)(2,1)}, bf16[256,256]{1,0:T(8,128)(2,1)}, f32[256,256]{1,0:T(8,128)}, /*index=5*/f32[1,256]{1,0:T(1,128)}) custom-call(bf16[256,256]{1,0:T(8,128)(2,1)} %get-tuple-element.18.refs_0_, bf16[256,256]{1,0:T(8,128)(2,1)} %get-tuple-element.19.refs_1_, ...), custom_call_target="tpu_custom_call" | custom-call | tf_op jit(solution)/shard_map/hand_on/pallas_call | solution.py:320

commit v4 on v3

--- a/solution.py
+++ b/solution.py
@@ -16,8 +16,9 @@
 TILE = 8
 OWNERS = 2 * PLANE
 UNIT = 6
-MESSAGE = 4 * UNIT
-ROWS = OWNERS * MESSAGE
+FAR_FIRST = (2, 1, 3, 0)
+SPAN = OWNERS * TILE
+ROWS = 4 * SPAN
 
 
 def tables():
@@ -47,8 +48,23 @@
     return jnp.dot(a, b, preferred_element_type=F32)
 
 
-def dot3(a, b):
-    return dot(a[0], b[0]) + (dot(a[0], b[1]) + dot(a[1], b[0]))
+def dot_left(first, second, x):
+    high, low = split(x)
+    return dot(first, jnp.concatenate([high, high], 0)) + dot(second, low)
+
+
+def dot_right(x, high_table, low_table):
+    high, low = split(x)
+    count = x.shape[0]
+    both = dot(jnp.concatenate([high, low], 0), high_table)
+    return both[:count] + (both[count:] + dot(high, low_table))
+
+
+def dot_stacked(both_tables, high_table, x):
+    high, low = split(x)
+    both = dot(both_tables, high)
+    count = high_table.shape[0]
+    return both[:count] + (both[count:] + dot(high_table, low))
 
 
 def kernel(
@@ -58,9 +74,9 @@
     q, k, v, taps, skip, cot,
     f1, f2, g1, g2, tr, ti,
     gated, gq, gk, gv, gt, gs,
-    sa, sb, ra, rb,
-    skip_send, skip_recv, f1h, f1l, f2h, f2l, g1h, g1l, g2h, g2l,
-    load_sem, store_sem, send_sem, recv_sem, sk_send, sk_recv,
+    sa, sb, ra, rb, ea,
+    skip_send, skip_recv, f1h, f1b, f2h, f2l, g1h, g1b, g2h, g2l,
+    load_sem, store_sem, send_sem, recv_sem, sk_send, sk_recv, over_send, over_recv, column_sem, core_sem, plane_sem,
 ):
     ctx = lax.axis_index("ctx")
     core, mz, yx = ctx % 2, (ctx // 2) % 2, ctx // 4
@@ -77,59 +93,105 @@
         dx = jnp.where(t >= 4, 3 - a % 4, a % 4)
         return ((y + dy) % 4 * 4 + (x + dx) % 4) * 2 + (core + 1 - t % 2) % 2
 
+    def to_plane(action, z, self_too=False):
+        for dy in FAR_FIRST:
+
+            def body(t, carry, dy=dy):
+                action(z, peer(dy, t))
+                return carry
+
+            lax.fori_loop(0, 8 if self_too or dy else 7, body, 0)
+
     def to_others(action):
-        for z in (oz, mz):
-            for dy in (2, 1, 3, 0):
-
-                def body(t, carry, z=z, dy=dy):
-                    action(z, peer(dy, t))
-                    return carry
-
-                lax.fori_loop(0, 7 if z is mz and dy == 0 else 8, body, 0)
+        to_plane(action, oz, True)
+        to_plane(action, mz)
 
     z_device = {"ctx": yx * 4 + oz * 2 + core}
+    core_device = {"ctx": yx * 4 + mz * 2 + 1 - core}
+    row = [{"ctx": (y * 4 + (x + d) % 4) * 4 + mz * 2 + core} for d in (2, 1, 3)]
+    column = [{"ctx": ((y + d) % 4 * 4 + x) * 4 + mz * 2 + core} for d in (2, 1, 3)]
+
+    def signal(sem, devices):
+        for target in devices:
+            pl.semaphore_signal(sem, inc=1, device_id=target, device_id_type=MESH)
 
     def part(owner, c):
-        return pl.ds(pl.multiple_of(owner * MESSAGE, TILE) + c * UNIT, UNIT)
+        return pl.ds(pl.multiple_of(c * SPAN + owner * TILE, TILE), UNIT)
 
     barrier = pltpu.get_barrier_semaphore()
-
-    def greet(z, p):
-        pl.semaphore_signal(barrier, inc=1, device_id=device(z, p), device_id_type=MESH)
 
     sources = (k_in, v_in, taps_in, q_in, cot_in, f1_in, f2_in, g2_in, g1_in, tr_in, ti_in, skip_in)
     targets = (k, v, taps, q, cot, f1, f2, g2, g1, tr, ti, skip)
     loads = [pltpu.make_async_copy(s, t, load_sem.at[i]) for i, (s, t) in enumerate(zip(sources, targets))]
-    to_others(greet)
-    for load in loads:
+    for load in loads[:5]:
+        load.start()
+    signal(barrier, [z_device, *column, *row, core_device])
+    for load in loads[5:]:
         load.start()
 
     def wait_rows(ref, count, sem):
         pltpu.make_async_copy(ref.at[pl.ds(0, count)], ref.at[pl.ds(0, count)], sem).wait()
 
-    def send(i, c, src, dst):
-        mine = part(mz * PLANE + me, c)
-
-        def one(z, p):
-            pltpu.make_async_remote_copy(
-                src_ref=src.at[part(z * PLANE + p, c)],
-                dst_ref=dst.at[mine],
-                send_sem=send_sem.at[i],
-                recv_sem=recv_sem.at[i],
-                device_id=device(z, p),
-                device_id_type=MESH,
-            ).start()
-
-        to_others(one)
-        dst[mine, :] = src[mine, :]
-
-    def arrived(i, r):
-        wait_rows(r, (OWNERS - 1) * UNIT, recv_sem.at[i])
+    def give(src, at, dst, i, c, z, p, source):
+        pltpu.make_async_remote_copy(
+            src_ref=src.at[at],
+            dst_ref=dst.at[part(source * PLANE + me, c)],
+            send_sem=send_sem.at[i],
+            recv_sem=recv_sem.at[i],
+            device_id=device(z, p),
+            device_id_type=MESH,
+        ).start()
+
+    def keep(src, at, dst, c, source):
+        dst[part(source * PLANE + me, c), :] = src[at, :]
+
+    def parked(p, c):
+        return pl.ds(pl.multiple_of((c * PLANE + p) * TILE, TILE), UNIT)
+
+    def cross(c):
+        for k, dy in enumerate(FAR_FIRST):
+
+            def one(t, carry, k=k, dy=dy):
+                p = peer(dy, t)
+                pltpu.make_async_remote_copy(
+                    src_ref=sa.at[part(oz * PLANE + p, c)],
+                    dst_ref=ea.at[parked(p, c)],
+                    send_sem=over_send.at[c],
+                    recv_sem=over_recv.at[c, k],
+                    device_id=z_device,
+                    device_id_type=MESH,
+                ).start()
+                return carry
+
+            lax.fori_loop(0, 8, one, 0)
+
+    def own_plane(c):
+        to_plane(lambda z, p: give(sa, part(z * PLANE + p, c), ra, c, c, z, p, mz), mz)
+        keep(sa, part(mz * PLANE + me, c), ra, c, mz)
+
+    def hand_over(c):
+        for k, dy in enumerate(FAR_FIRST):
+            wait_rows(ea, 8 * UNIT, over_recv.at[c, k])
+
+            def one(t, carry, dy=dy):
+                p = peer(dy, t)
+                give(ea, parked(p, c), ra, c, c, mz, p, oz)
+                return carry
+
+            lax.fori_loop(0, 8 if dy else 7, one, 0)
+        keep(ea, parked(me, c), ra, c, oz)
+
+    def back(c):
+        to_others(lambda z, p: give(sb, part(z * PLANE + p, c), rb, 4 + c, c, z, p, mz))
+        keep(sb, part(mz * PLANE + me, c), rb, c, mz)
+
+    def moved(i, sem):
+        wait_rows(ra, (OWNERS - 1 - (i < 4)) * UNIT, sem.at[i])
 
     def put(s, pair, field, values, h):
         flipped = values.T
         for c in range(2):
-            s[pl.ds((pair * 2 + c) * UNIT + field * 2 + h, OWNERS, stride=MESSAGE), :] = flipped[
+            s[pl.ds((pair * 2 + c) * SPAN + field * 2 + h, OWNERS, stride=TILE), :] = flipped[
                 c * OWNERS : (c + 1) * OWNERS
             ]
 
@@ -143,21 +205,21 @@
             put(s, pair, 2, piece(q, h, pair) * piece(cot, h, pair), h)
 
     def series_rows(c, field, h, z):
-        return pl.ds(z * PLANE * MESSAGE + c * UNIT + field * 2 + h, PLANE, stride=MESSAGE)
+        return pl.ds(c * SPAN + z * PLANE * TILE + field * 2 + h, PLANE, stride=TILE)
 
     def transform(c):
         series = []
         for field in range(3):
             parts = [ra[series_rows(c, field, h, z), :] for h in range(2) for z in range(2)]
             series.append(jnp.concatenate(parts, 0))
-        a = dot3((f1h[...], f1l[...]), split(jnp.concatenate(series, 1)))
+        a = dot_left(f1b[...], f1h[...], jnp.concatenate(series, 1))
         tc, ts = tr[...], ti[...]
         turned = []
         for field in range(3):
             cols = slice(field * HALF, (field + 1) * HALF)
             ar, ai = a[:HALF, cols], a[HALF:, cols]
             turned.append(jnp.concatenate([ar * tc - ai * ts, ar * ts + ai * tc], 1))
-        b = dot3(split(jnp.concatenate(turned, 0)), (f2h[...], f2l[...]))
+        b = dot_right(jnp.concatenate(turned, 0), f2h[...], f2l[...])
         (ur, ui), (hr, hi), (gr, gi) = [
             (b[f * HALF : (f + 1) * HALF, :HALF], b[f * HALF : (f + 1) * HALF, HALF:]) for f in range(3)
         ]
@@ -169,13 +231,13 @@
             ],
             0,
         )
-        d = dot3(split(prods), (g2h[...], g2l[...]))
+        d = dot_right(prods, g2h[...], g2l[...])
         turned = []
         for field in range(3):
             at = slice(field * HALF, (field + 1) * HALF)
             dr, di = d[at, :HALF], d[at, HALF:]
             turned.append(jnp.concatenate([dr * tc + di * ts, di * tc - dr * ts], 0))
-        out = dot3((g1h[...], g1l[...]), split(jnp.concatenate(turned, 1)))
+        out = dot_stacked(g1b[...], g1h[...], jnp.concatenate(turned, 1))
         for field in range(3):
             for h in range(2):
                 for z in range(2):
@@ -186,7 +248,7 @@
 
     def take(pair, field, h):
         parts = [
-            rb[pl.ds((pair * 2 + c) * UNIT + field * 2 + h, OWNERS, stride=MESSAGE), :] for c in range(2)
+            rb[pl.ds((pair * 2 + c) * SPAN + field * 2 + h, OWNERS, stride=TILE), :] for c in range(2)
         ]
         return jnp.concatenate(parts, 0).T
 
@@ -216,11 +278,20 @@
 
     for i in range(5):
         loads[i].wait()
-    for pair in range(2):
-        lay_out(sa, pair)
-    pl.semaphore_wait(barrier, OWNERS - 1)
+    lay_out(sa, 0)
+    pl.semaphore_wait(barrier, 8)
+    cross(0)
+    cross(1)
+    signal(column_sem, column)
+    lay_out(sa, 1)
+    cross(2)
+    cross(3)
+    pl.semaphore_wait(column_sem, 3)
+    signal(core_sem, [core_device])
+    pl.semaphore_wait(core_sem, 1)
+    signal(plane_sem, [z_device])
     for c in range(4):
-        send(c, c, sa, ra)
+        own_plane(c)
     total = jnp.zeros((TILE, 2 * HALF), F32)
     for i in range(4):
         at = slice(i * 64, (i + 1) * 64)
@@ -230,13 +301,22 @@
     skip_copy(0).start()
     for i in range(5, len(loads)):
         loads[i].wait()
-    for table, high, low in ((f1, f1h, f1l), (f2, f2h, f2l), (g2, g2h, g2l), (g1, g1h, g1l)):
+    for table, high, low in ((f2, f2h, f2l), (g2, g2h, g2l)):
         high[...], low[...] = split(table[...])
+    high, low = split(f1[...])
+    f1h[...], f1b[...] = high, jnp.concatenate([high, low], 1)
+    high, low = split(g1[...])
+    g1h[...], g1b[...] = high, jnp.concatenate([high, low], 0)
     skip_step(0)
+    hand_over(0)
     for c in range(4):
-        arrived(c, ra)
+        if c < 3:
+            hand_over(c + 1)
+        moved(c, recv_sem)
         transform(c)
-        send(4 + c, c, sb, rb)
+        if c == 0:
+            pl.semaphore_wait(plane_sem, 1)
+        back(c)
         skip_step(c + 1)
 
     def finish(pair):
@@ -259,16 +339,18 @@
             zip((gated, gq, gs, gk, gv, gt), (gated_out, gq_out, gs_out, gk_out, gv_out, gt_out))
         )
     ]
-    arrived(4, rb)
-    arrived(5, rb)
+    moved(4, recv_sem)
+    moved(5, recv_sem)
     finish(0)
     skip_step(5)
+    for c in range(4):
+        wait_rows(ea, PLANE * UNIT, over_send.at[c])
     for i in range(8):
-        wait_rows(ra, (OWNERS - 1) * UNIT, send_sem.at[i])
+        moved(i, send_sem)
     for i in range(len(partners)):
         skip_copy(i).wait_send()
-    arrived(6, rb)
-    arrived(7, rb)
+    moved(6, recv_sem)
+    moved(7, recv_sem)
     finish(1)
     for store in stores:
         store.start()
@@ -309,9 +391,14 @@
         scratch_shapes=[pltpu.VMEM(a.shape, a.dtype) for a in args]
         + [pltpu.VMEM(o.shape, o.dtype) for o in outs]
         + [vmem(ROWS, HALF)] * 4
+        + [vmem(4 * PLANE * TILE, HALF)]
         + [vmem(6, TILE, 2 * HALF)] * 2
-        + [pltpu.VMEM(s, BF16) for s in ((256, 128), (256, 256), (128, 256), (256, 256)) for _ in range(2)]
-        + [dma((12,)), dma((6,)), dma((8,)), dma((8,)), dma((6,)), dma((6,))],
+        + [
+            pltpu.VMEM(s, BF16)
+            for s in ((256, 128), (256, 256), (256, 256), (256, 256), (128, 256), (256, 256), (256, 256), (256, 256))
+        ]
+        + [dma((12,)), dma((6,)), dma((8,)), dma((8,)), dma((6,)), dma((6,)), dma((4,)), dma((4, 4))]
+        + [pltpu.SemaphoreType.REGULAR] * 3,
         compiler_params=pltpu.CompilerParams(
             collective_id=0, has_side_effects=True, vmem_limit_bytes=56 * 1024 * 1024
         ),

time: 53.6 us -> 52.2 us (0.974)
  Pallas kernels: 52.9 us -> 51.4 us
    pallas_call x1, Pallas kernels: 50.8 us -> 49.4 us  [shards(): pl.pallas_call(kernel, out_shape=outs, in_specs=[anywhere] * len(args), o...]
where the time goes in v4:
time: 52.2 us; the launch traced here: 52.1 us
  Pallas kernels  51.4 us (98%)
  between operations  0.64 us (1%)
    pallas_call x1, Pallas kernels, shards(): pl.pallas_call(kernel, out_shape=outs, in_specs=[anywhere] * len(args), o...  49.4 us
    pallas_call x1, Pallas kernels, shards(): pl.pallas_call(hand_on, out_shape=outs, in_specs=[anywhere] * len(outs),...  2.02 us

profile of v4, /device:TPU:33, one launch (start us, length us, event | category | flops | bytes accessed | tf_op | source)
XLA Modules:
  0.0 52.1 jit_solution(9032933899961020063)
XLA Ops:
  0.6 49.4 %long_conv.1 = (bf16[256,256]{1,0:T(8,128)(2,1)}, bf16[256,256]{1,0:T(8,128)(2,1)}, bf16[256,256]{1,0:T(8,128)(2,1)}, bf16[256,256]{1,0:T(8,128)(2,1)}, f32[256,256]{1,0:T(8,128)}, /*index=5*/f32[1,256]{1,0:T(1,128)}) custom-call(bf16[256,256]{1,0:T(8,128)(2,1)} %q_in.1, bf16[256,256]{1,0:T(8,128)(2,1)} %k_in.1, bf16[256,256]{1,0:T(8,128)(2,1)} %v_in.1, ...), custom_call_target="tpu_custom_call" | custom-call | tf_op jit(solution)/shard_map/long_conv/pallas_call | solution.py:386
  50.0 2.0 %hand_on.1 = (bf16[256,256]{1,0:T(8,128)(2,1)}, bf16[256,256]{1,0:T(8,128)(2,1)}, bf16[256,256]{1,0:T(8,128)(2,1)}, bf16[256,256]{1,0:T(8,128)(2,1)}, f32[256,256]{1,0:T(8,128)}, /*index=5*/f32[1,256]{1,0:T(1,128)}) custom-call(bf16[256,256]{1,0:T(8,128)(2,1)} %get-tuple-element.18.refs_0_, bf16[256,256]{1,0:T(8,128)(2,1)} %get-tuple-element.19.refs_1_, ...), custom_call_target="tpu_custom_call" | custom-call | tf_op jit(solution)/shard_map/hand_on/pallas_call | solution.py:407

commit v5 on v4

--- a/solution.py
+++ b/solution.py
@@ -70,13 +70,12 @@
 def kernel(
     q_in, k_in, v_in, taps_in, skip_in, cot_in,
     f1_in, f2_in, g1_in, g2_in, tr_in, ti_in,
-    gated_out, gq_out, gk_out, gv_out, gt_out, gs_out,
+    gated, gq, gk, gv, gt, gs,
     q, k, v, taps, skip, cot,
     f1, f2, g1, g2, tr, ti,
-    gated, gq, gk, gv, gt, gs,
     sa, sb, ra, rb, ea,
     skip_send, skip_recv, f1h, f1b, f2h, f2l, g1h, g1b, g2h, g2l,
-    load_sem, store_sem, send_sem, recv_sem, sk_send, sk_recv, over_send, over_recv, column_sem, core_sem, plane_sem,
+    load_sem, send_sem, recv_sem, sk_send, sk_recv, over_send, over_recv, column_sem, core_sem, plane_sem,
 ):
     ctx = lax.axis_index("ctx")
     core, mz, yx = ctx % 2, (ctx // 2) % 2, ctx // 4
@@ -181,12 +180,13 @@
             lax.fori_loop(0, 8 if dy else 7, one, 0)
         keep(ea, parked(me, c), ra, c, oz)
 
-    def back(c):
-        to_others(lambda z, p: give(sb, part(z * PLANE + p, c), rb, 4 + c, c, z, p, mz))
-        keep(sb, part(mz * PLANE + me, c), rb, c, mz)
+    def direct(src, dst, i, c):
+        to_others(lambda z, p: give(src, part(z * PLANE + p, c), dst, i, c, z, p, mz))
+        keep(src, part(mz * PLANE + me, c), dst, c, mz)
 
     def moved(i, sem):
-        wait_rows(ra, (OWNERS - 1 - (i < 4)) * UNIT, sem.at[i])
+        count = 2 * (PLANE - 1) if i < 3 else OWNERS - 1
+        wait_rows(ra, count * UNIT, sem.at[i])
 
     def put(s, pair, field, values, h):
         flipped = values.T
@@ -285,12 +285,11 @@
     signal(column_sem, column)
     lay_out(sa, 1)
     cross(2)
-    cross(3)
     pl.semaphore_wait(column_sem, 3)
     signal(core_sem, [core_device])
     pl.semaphore_wait(core_sem, 1)
     signal(plane_sem, [z_device])
-    for c in range(4):
+    for c in range(3):
         own_plane(c)
     total = jnp.zeros((TILE, 2 * HALF), F32)
     for i in range(4):
@@ -309,14 +308,14 @@
     g1h[...], g1b[...] = high, jnp.concatenate([high, low], 0)
     skip_step(0)
     hand_over(0)
+    pl.semaphore_wait(plane_sem, 1)
+    direct(sa, ra, 3, 3)
     for c in range(4):
-        if c < 3:
+        if c < 2:
             hand_over(c + 1)
         moved(c, recv_sem)
         transform(c)
-        if c == 0:
-            pl.semaphore_wait(plane_sem, 1)
-        back(c)
+        direct(sb, rb, 4 + c, c)
         skip_step(c + 1)
 
     def finish(pair):
@@ -333,17 +332,11 @@
             gv[at, cols] = (grad * kp).astype(BF16)
             gt[at, cols] = take(pair, 2, h) * (1.0 / HALF)
 
-    stores = [
-        pltpu.make_async_copy(s, t, store_sem.at[i])
-        for i, (s, t) in enumerate(
-            zip((gated, gq, gs, gk, gv, gt), (gated_out, gq_out, gs_out, gk_out, gv_out, gt_out))
-        )
-    ]
     moved(4, recv_sem)
     moved(5, recv_sem)
     finish(0)
     skip_step(5)
-    for c in range(4):
+    for c in range(3):
         wait_rows(ea, PLANE * UNIT, over_send.at[c])
     for i in range(8):
         moved(i, send_sem)
@@ -352,24 +345,15 @@
     moved(6, recv_sem)
     moved(7, recv_sem)
     finish(1)
-    for store in stores:
-        store.start()
-    for store in stores:
-        store.wait()
 
 
 def hand_on(*refs):
-    count = len(refs) // 3
-    into, out = refs[-2:]
-    reads = [pltpu.make_async_copy(refs[i], refs[2 * count + i], into.at[i]) for i in range(count)]
-    writes = [pltpu.make_async_copy(refs[2 * count + i], refs[count + i], out.at[i]) for i in range(count)]
-    for read in reads:
-        read.start()
-    for read, write in zip(reads, writes):
-        read.wait()
-        write.start()
-    for write in writes:
-        write.wait()
+    count = len(refs) // 2
+    copies = [pltpu.make_async_copy(refs[i], refs[count + i], refs[-1].at[i]) for i in range(count)]
+    for copy in copies:
+        copy.start()
+    for copy in copies:
+        copy.wait()
 
 
 def shards(query_proj, key_proj, value_proj, filter_taps, skip_bias, cotangent):
@@ -385,19 +369,18 @@
     dma = pltpu.SemaphoreType.DMA
     results = pl.pallas_call(
         kernel,
-        out_shape=outs,
+        out_shape=[pltpu.VMEM(o.shape, o.dtype) for o in outs],
         in_specs=[anywhere] * len(args),
-        out_specs=[anywhere] * len(outs),
+        out_specs=[pl.BlockSpec(memory_space=pltpu.VMEM)] * len(outs),
         scratch_shapes=[pltpu.VMEM(a.shape, a.dtype) for a in args]
-        + [pltpu.VMEM(o.shape, o.dtype) for o in outs]
         + [vmem(ROWS, HALF)] * 4
-        + [vmem(4 * PLANE * TILE, HALF)]
+        + [vmem(3 * PLANE * TILE, HALF)]
         + [vmem(6, TILE, 2 * HALF)] * 2
         + [
             pltpu.VMEM(s, BF16)
             for s in ((256, 128), (256, 256), (256, 256), (256, 256), (128, 256), (256, 256), (256, 256), (256, 256))
         ]
-        + [dma((12,)), dma((6,)), dma((8,)), dma((8,)), dma((6,)), dma((6,)), dma((4,)), dma((4, 4))]
+        + [dma((12,)), dma((8,)), dma((8,)), dma((6,)), dma((6,)), dma((3,)), dma((3, 4))]
         + [pltpu.SemaphoreType.REGULAR] * 3,
         compiler_params=pltpu.CompilerParams(
             collective_id=0, has_side_effects=True, vmem_limit_bytes=56 * 1024 * 1024
@@ -407,12 +390,12 @@
     gated, grad_query, grad_key, grad_value, grad_taps, grad_skip = pl.pallas_call(
         hand_on,
         out_shape=outs,
-        in_specs=[anywhere] * len(outs),
+        in_specs=[pl.BlockSpec(memory_space=pltpu.VMEM)] * len(outs),
         out_specs=[anywhere] * len(outs),
-        scratch_shapes=[pltpu.VMEM(o.shape, o.dtype) for o in outs] + [dma((len(outs),))] * 2,
+        scratch_shapes=[dma((len(outs),))],
         compiler_params=pltpu.CompilerParams(vmem_limit_bytes=56 * 1024 * 1024),
         name="hand_on",
-    )(*results)
+    )(*[pltpu.with_memory_space_constraint(r, pltpu.VMEM) for r in results])
     return gated, grad_query, grad_key, grad_value, grad_taps, grad_skip.reshape(-1)
 
 

time: 52.2 us -> 49.2 us (0.943)
  Pallas kernels: 51.4 us -> 48.5 us
    pallas_call x2, Pallas kernels: 51.4 us -> 48.5 us  [the longest x1 47.5 us: shards(): pl.pallas_call(kernel, out_shape=[pltpu.VMEM(o.shape, o.dtype) for o in o...]
where the time goes in v5:
time: 49.2 us; the launch traced here: 49.1 us
  Pallas kernels  48.5 us (99%)
  between operations  0.64 us (1%)
    pallas_call x1, Pallas kernels, shards(): pl.pallas_call(kernel, out_shape=[pltpu.VMEM(o.shape, o.dtype) for o in o...  47.5 us

profile of v5, /device:TPU:33, one launch (start us, length us, event | category | flops | bytes accessed | tf_op | source)
XLA Modules:
  0.0 49.1 jit_solution(4285241915405988714)
XLA Ops:
  0.6 47.5 %long_conv.1 = (bf16[256,256]{1,0:T(8,128)(2,1)S(1)}, bf16[256,256]{1,0:T(8,128)(2,1)S(1)}, bf16[256,256]{1,0:T(8,128)(2,1)S(1)}, bf16[256,256]{1,0:T(8,128)(2,1...) custom-call(bf16[256,256]{1,0:T(8,128)(2,1)} %q_in.1, bf16[256,256]{1,0:T(8,128)(2,1)} %k_in.1, ...), custom_call_target="tpu_custom_call" | custom-call | tf_op jit(solution)/shard_map/long_conv/pallas_call | solution.py:370
  48.2 0.9 %hand_on.1 = (bf16[256,256]{1,0:T(8,128)(2,1)}, bf16[256,256]{1,0:T(8,128)(2,1)}, bf16[256,256]{1,0:T(8,128)(2,1)}, bf16[256,256]{1,0:T(8,128)(2,1)}, f32[256,256]{1,0:T(8,128)}, /*index=5*/f32[1,256]{1,0:T(1,128)}) custom-call(bf16[256,256]{1,0:T(8,128)(2,1)S(1)} %get-tuple-element.18.refs_0_, bf16[256,256]{1,0:T(8,128)(2,1)S(1)} %get-tuple-element.19.refs_1_, ...), custom_call_target="tpu_custom_call" | custom-call | tf_op jit(solution)/shard_map/hand_on/pallas_call | solution.py:390

commit v6 on v5

--- a/solution.py
+++ b/solution.py
@@ -102,8 +102,16 @@
             lax.fori_loop(0, 8 if self_too or dy else 7, body, 0)
 
     def to_others(action):
-        to_plane(action, oz, True)
-        to_plane(action, mz)
+        for dy in FAR_FIRST:
+
+            def body(t, carry, dy=dy):
+                p = peer(dy, t)
+                action(oz, p)
+                action(mz, p)
+                return carry
+
+            lax.fori_loop(0, 8 if dy else 7, body, 0)
+        action(oz, me)
 
     z_device = {"ctx": yx * 4 + oz * 2 + core}
     core_device = {"ctx": yx * 4 + mz * 2 + 1 - core}

time: 49.2 us -> 48.8 us (level)
  no operation moved by 1% of the time
where the time goes in v6:
time: 48.8 us; the launch traced here: 48.7 us
  Pallas kernels  48.1 us (99%)
  between operations  0.64 us (1%)
    pallas_call x1, Pallas kernels, shards(): pl.pallas_call(kernel, out_shape=[pltpu.VMEM(o.shape, o.dtype) for o in o...  47.2 us

profile of v6, /device:TPU:33, one launch (start us, length us, event | category | flops | bytes accessed | tf_op | source)
XLA Modules:
  0.0 48.7 jit_solution(4600600864301697773)
XLA Ops:
  0.6 47.2 %long_conv.1 = (bf16[256,256]{1,0:T(8,128)(2,1)S(1)}, bf16[256,256]{1,0:T(8,128)(2,1)S(1)}, bf16[256,256]{1,0:T(8,128)(2,1)S(1)}, bf16[256,256]{1,0:T(8,128)(2,1...) custom-call(bf16[256,256]{1,0:T(8,128)(2,1)} %q_in.1, bf16[256,256]{1,0:T(8,128)(2,1)} %k_in.1, ...), custom_call_target="tpu_custom_call" | custom-call | tf_op jit(solution)/shard_map/long_conv/pallas_call | solution.py:378
  47.8 0.9 %hand_on.1 = (bf16[256,256]{1,0:T(8,128)(2,1)}, bf16[256,256]{1,0:T(8,128)(2,1)}, bf16[256,256]{1,0:T(8,128)(2,1)}, bf16[256,256]{1,0:T(8,128)(2,1)}, f32[256,256]{1,0:T(8,128)}, /*index=5*/f32[1,256]{1,0:T(1,128)}) custom-call(bf16[256,256]{1,0:T(8,128)(2,1)S(1)} %get-tuple-element.18.refs_0_, bf16[256,256]{1,0:T(8,128)(2,1)S(1)} %get-tuple-element.19.refs_1_, ...), custom_call_target="tpu_custom_call" | custom-call | tf_op jit(solution)/shard_map/hand_on/pallas_call | solution.py:398
